TPU v7x, 1024 devices: a whole 4x4x32 slice. The times are simulated.
1024 devices in a mesh: expert: 64 (over z, core), tensor: 16 (over x, y).
Axes of the slice: x: 4, y: 4, z: 32, core: 2. Of those that a mesh axis runs over, the one named last changes fastest.
Arguments:
- cotangent: bfloat16 [4096, 4096], P('expert', 'tensor'), may hold values from -6 to 6
- activations: bfloat16 [4096, 4096], P('expert', 'tensor'), may hold values from -6 to 6
- router_logits: float32 [4096, 16], P('expert'), may hold values from -195 to 195
- saved_hidden: bfloat16 [512, 262144], P(None, ('expert', 'tensor')), may hold values from -0.046875 to 0.046875
- down_weight: bfloat16 [262144, 4096], P(('expert', 'tensor')), may hold values from -0.09375 to 0.09375
- router_weight: bfloat16 [4096, 16], P('tensor'), may hold values from -1.5 to 1.5
- choices: int32 [16, 512], replicated, may hold values from 0 to 4095, as said below
Outputs:
- hidden_grad: bfloat16 [512, 262144], P(None, ('expert', 'tensor'))
- token_grad: bfloat16 [4096, 4096], P('expert', 'tensor')
- router_grad: float32 [4096, 16], P('tensor')
Inputs may be any that keep to these rules, and one draw needn't show every extreme that they name: `choices`: each row names 512 different tokens. Of the 64 tokens o * 64 to (o + 1) * 64 - 1 of one index o of expert, a row names at most 16, and every row names exactly 16 from some index.
All inputs are finite; a program needn't handle non-finite values.
Results may differ from a plain program's by a relative error of at most 0.0075.
Values may be sent and summed in bfloat16 or wider, within the bound.
A program may use at most 32 MiB of HBM per device.

v0:
```python
import jax
import jax.numpy as jnp
from jax import lax
from jax.sharding import PartitionSpec as P


def on_device(
    cotangent, activations, router_logits, saved_hidden, down_weight, router_weight, choices
):
    groups = lax.axis_size("expert")
    owner_index = lax.axis_index("expert")
    own_tokens = cotangent.shape[0]
    experts = choices.shape[0]
    capacity = choices.shape[1]
    quarter = groups // experts
    expert = owner_index // quarter
    expert_rows = lax.dynamic_index_in_dim(choices, expert, 0, keepdims=False)
    router_probs = jax.nn.softmax(router_logits, axis=1)
    probs_bf = router_probs.astype(jnp.bfloat16)
    feature_cols = cotangent.shape[1]
    start_state = (
        jnp.zeros((capacity, feature_cols), jnp.bfloat16),
        jnp.zeros((capacity,), jnp.bfloat16),
    )
    block_rows = lax.all_gather(cotangent, "expert", axis=0, tiled=True)
    block_probs = lax.all_gather(probs_bf, "expert", axis=0, tiled=True)
    local_rows = expert_rows
    inside = (local_rows >= 0) & (local_rows < block_rows.shape[0])
    safe_rows = jnp.clip(local_rows, 0, block_rows.shape[0] - 1)
    fetched = block_rows[safe_rows]
    weight = lax.dynamic_index_in_dim(block_probs[safe_rows], expert, 1, keepdims=False)
    picked = jnp.where(inside[:, None], fetched, start_state[0])
    gate_bf = jnp.where(inside, weight, start_state[1])
    pre_gate = lax.dot_general(
        lax.all_gather(picked, "tensor", axis=1, tiled=True),
        down_weight,
        (((1,), (1,)), ((), ())),
        preferred_element_type=jnp.float32,
    )
    gate_part = jnp.sum(saved_hidden.astype(jnp.float32) * pre_gate, axis=1)
    gate_part = lax.psum(gate_part, "tensor")
    hidden_grad = (gate_bf.astype(jnp.float32)[:, None] * pre_gate).astype(jnp.bfloat16)
    all_parts = lax.all_gather(gate_part[None, :], "expert", axis=0, tiled=True)
    summed = all_parts.reshape(experts, quarter, capacity).sum(axis=1)
    local_rows = choices - owner_index * own_tokens
    is_mine = (local_rows >= 0) & (local_rows < own_tokens)
    safe_rows = jnp.clip(local_rows, 0, own_tokens - 1)
    expert_ids = jnp.broadcast_to(
        jnp.arange(experts, dtype=jnp.int32)[:, None], (experts, capacity)
    )
    score_grad = (
        jnp.zeros((own_tokens, experts), jnp.float32)
        .at[safe_rows, expert_ids]
        .add(jnp.where(is_mine, summed, 0.0))
    )
    inner_sum = jnp.sum(router_probs * score_grad, axis=1, keepdims=True)
    logit_grad = (router_probs * (score_grad - inner_sum)).astype(jnp.bfloat16)
    token_grad = lax.dot_general(
        logit_grad, router_weight, (((1,), (1,)), ((), ())), preferred_element_type=jnp.float32
    ).astype(jnp.bfloat16)
    router_part = lax.dot_general(
        activations, logit_grad, (((0,), (0,)), ((), ())), preferred_element_type=jnp.float32
    )
    router_grad = lax.psum(router_part, "expert")
    return (hidden_grad, token_grad, router_grad)


def solution(mesh):
    placed = (
        P("expert", "tensor"),
        P("expert", "tensor"),
        P("expert", None),
        P(None, ("expert", "tensor")),
        P(("expert", "tensor"), None),
        P("tensor", None),
        P(),
    )
    return jax.shard_map(
        on_device,
        mesh=mesh,
        in_specs=placed,
        out_specs=(P(None, ("expert", "tensor")), P("expert", "tensor"), P("tensor", None)),
        check_vma=False,
    )
```

profile of v0, /device:TPU:1, one launch (start us, length us, event | category | flops | bytes accessed | tf_op | source)
XLA Modules:
  0.0 588.8 jit_solution(17808234629367294213)
XLA Ops:
  7.2 0.0 copy-start
  7.2 0.0 copy-start.1
  7.2 0.0 all-gather.5.cloned.1.call-start
  7.2 0.7 all-gather.5.cloned.1.call-update
  7.9 0.0 all-gather.7.cloned.1.call-start
  8.0 0.7 compare_select_fusion.1
  8.7 1.3 fusion.8
  10.0 146.4 %all-gather.5.cloned.1.call-done = bf16[4096,256]{1,0:T(8,128)(2,1)} async-done(((bf16[64,256]{1,0:T(8,128)(2,1)}), bf16[4096,256]{1,0:T(8,128)(2,1)}) %all-gather.5.cloned.1.call-update) | async-done | bytes 2097168 | tf_op jit(solution)/shard_map/all_gather | solution.py:25
  156.4 3.4 gather_fusion.1
  159.9 0.8 broadcast_select_fusion
  160.7 0.0 all-gather.7.cloned.1.call-update
  160.7 0.0 copy-done.1
  160.8 0.0 copy-start.5
  160.8 0.5 copy-done.5
  161.3 54.4 %all-gather = bf16[64,64,16]{1,2,0:T(8,128)(2,1)S(1)} all-gather(bf16[1,64,16]{1,2,0:T(8,128)(2,1)S(1)} %convert_bitcast_fusion), channel_id=1, replica_groups=mesh['expert'=64,'tensor'=16] {'expert'}, dimensions={0}, use_global_device_ids=true | all-gather | bytes 133120 | tf_op jit(solution)/shard_map/all_gather | solution.py:26
  215.7 0.5 copy.17
  216.2 1.3 gather_fusion
  217.5 0.9 copy.18
  218.4 1.1 copy.19
  219.5 0.8 fusion
  220.3 0.7 multiply_reduce_fusion.1
  221.0 0.7 and_reduce_fusion
  221.8 0.2 convert_reduce_fusion
  222.0 0.0 copy-start.2
  222.0 0.0 copy-start.6
  222.0 0.0 copy-start.4
  222.1 0.0 copy-start.3
  222.1 22.4 %all-gather.7.cloned.1.call-done = bf16[512,4096]{1,0:T(8,128)(2,1)} async-done(((bf16[512,256]{1,0:T(8,128)(2,1)}), bf16[512,4096]{1,0:T(8,128)(2,1)}) %all-gather.7.cloned.1.call-update) | async-done | bytes 4194320 | tf_op jit(solution)/shard_map/all_gather | solution.py:35
  244.5 0.0 copy-done
  244.5 3.5 multiply_reduce_fusion
  248.0 30.9 %psum.14 = f32[1,512]{1,0:T(1,128)S(1)} all-reduce(f32[1,512]{1,0:T(1,128)S(1)} %bitcast.40), channel_id=1, replica_groups=mesh['expert'=64,'tensor'=16] {'tensor'}, use_global_device_ids=true, to_apply=%region_3.4 | all-reduce | flops 512 | bytes 4096 | tf_op jit(solution)/shard_map/psum | solution.py:41
  278.9 67.1 %all-gather.1 = f32[64,1,512]{2,1,0:T(1,128)S(1)} all-gather(f32[1,1,512]{2,1,0:T(1,128)S(1)} %bitcast.37), channel_id=1, replica_groups=mesh['expert'=64,'tensor'=16] {'expert'}, dimensions={0}, use_global_device_ids=true | all-gather | bytes 133120 | tf_op jit(solution)/shard_map/all_gather | solution.py:43
  346.1 0.3 reduce.4
  346.4 0.1 reduce_sum.38
  346.5 0.0 copy-done.2
  346.5 57.0 %scatter_custom_fusion = f32[1024]{0:T(1024)S(1)} fusion(s32[8192]{0:T(1024)S(1)} %bitcast.35, f32[8192]{0:T(1024)S(1)} %bitcast.36, f32[]{:T(128)} %constant.49.clone.1), kind=kCustom, calls=%fused_computation.28 | custom fusion | flops 8192 | bytes 4100
  403.6 0.1 reshape.84
  403.6 0.0 copy-done.6
  403.7 0.0 copy-done.4
  403.7 0.8 convolution_convert_fusion
  404.5 0.0 copy-done.3
  404.5 0.1 convolution_bitcast_fusion
  404.6 176.5 %psum.15 = f32[256,16]{0,1:T(8,128)} all-reduce(f32[256,16]{0,1:T(8,128)S(1)} %convolution_bitcast_fusion), channel_id=1, replica_groups=mesh['expert'=64,'tensor'=16] {'expert'}, use_global_device_ids=true, to_apply=%region_7.8 | all-reduce | flops 4096 | bytes 32768 | tf_op jit(solution)/shard_map/psum | solution.py:64
  581.1 0.8 copy.20
  (12 shorter events, 0.2 us)
Async XLA Ops:
  7.2 237.3 %copy-start = (bf16[256,4096]{1,0:T(8,128)(2,1)S(1)}, bf16[256,4096]{1,0:T(8,128)(2,1)}, u32[]{:S(2)}) copy-start(bf16[256,4096]{1,0:T(8,128)(2,1)} %param.11) | copy-start | bytes 6291460
  7.2 153.6 %copy-start.1 = (f32[64,16]{0,1:T(8,128)S(1)}, f32[64,16]{0,1:T(8,128)}, u32[]{:S(2)}) copy-start(f32[64,16]{0,1:T(8,128)} %param.9) | copy-start | bytes 12292
  7.2 149.3 %all-gather.5.cloned.1.call-start = ((), (), s32[]{:S(2)}) async-start(), calls=%async_computation | async-start | bytes 2129920 | tf_op jit(solution)/shard_map/all_gather | solution.py:25
  7.9 236.6 %all-gather.7.cloned.1.call-start = ((), (), s32[]{:S(2)}) async-start(), calls=%async_computation.1 | async-start | bytes 4456448 | tf_op jit(solution)/shard_map/all_gather | solution.py:35
  160.8 0.5 copy-start.5
  222.0 124.5 %copy-start.2 = (s32[16,512]{1,0:T(8,128)S(1)}, s32[16,512]{1,0:T(8,128)}, u32[]{:S(2)}) copy-start(s32[16,512]{1,0:T(8,128)} %param.13) | copy-start | bytes 98308
  222.0 181.6 %copy-start.6 = (f32[64]{0:T(128)S(1)}, f32[64]{0:T(128)}, u32[]{:S(2)}) copy-start(f32[64]{0:T(128)} %copy-done.5) | copy-start | bytes 772
  222.0 181.6 %copy-start.4 = (bf16[256,16]{0,1:T(8,128)(2,1)S(1)}, bf16[256,16]{0,1:T(8,128)(2,1)}, u32[]{:S(2)}) copy-start(bf16[256,16]{0,1:T(8,128)(2,1)} %param.12) | copy-start | bytes 24580
  222.1 182.4 %copy-start.3 = (bf16[64,256]{1,0:T(8,128)(2,1)S(1)}, bf16[64,256]{1,0:T(8,128)(2,1)}, u32[]{:S(2)}) copy-start(bf16[64,256]{1,0:T(8,128)(2,1)} %param.8) | copy-start | bytes 98308
Sparse Core Ops, SparseCore 0:
  10.7 145.6 all-gather.4
  161.2 83.2 all-gather.6
where the time goes:
time: 589 us
  blocking collectives  329 us (56%)
  waiting for transfers between devices  170 us (29%)
  other arithmetic  62.9 us (11%)
  between operations  14.3 us (2%)
  local copies, waits for them, and re-layouts  8.7 us (1%)
    psum x1, blocking collectives, on_device(): router_grad = lax.psum(router_part, 'expert')  177 us
    all_gather x1, waiting for transfers between devices, on_device(): block_rows = lax.all_gather(cotangent, 'expert', axis=0, tiled=True)  146 us
    all_gather x1, blocking collectives, on_device(): all_parts = lax.all_gather(gate_part[None, :], 'expert', axis=0, tiled=True)  67.1 us
    unnamed x6, other arithmetic  58.5 us
    all_gather x1, blocking collectives, on_device(): block_probs = lax.all_gather(probs_bf, 'expert', axis=0, tiled=True)  54.4 us
    psum x1, blocking collectives, on_device(): gate_part = lax.psum(gate_part, 'tensor')  30.9 us
    all_gather x1, waiting for transfers between devices, on_device(): lax.all_gather(picked, 'tensor', axis=1, tiled=True)  22.4 us
  transfers between devices with their start and end apart: 2, of which 2 were waited for; matrix products, arithmetic and copies ran while one was open for 1% of the time, Pallas kernels for 0%

commit v1 on v0

v1 whole, which is shorter than its diff:
```python
import functools

import jax
import jax.numpy as jnp
from jax import lax
from jax.experimental import pallas as pl
from jax.experimental.pallas import tpu as pltpu
from jax.sharding import PartitionSpec as P

MESH = pl.DeviceIdType.MESH
F32 = jnp.float32
BF16 = jnp.bfloat16
I32 = jnp.int32
SLOTS = 16
SIDE = 4
LANES = 128
NT = (((1,), (1,)), ((), ()))
TN = (((0,), (0,)), ((), ()))
NN = (((1,), (0,)), ((), ()))


def iota(shape, axis):
    return lax.broadcasted_iota(I32, shape, axis)


def dot(a, b, dims=NN, precision=None):
    return lax.dot_general(a, b, dims, precision=precision, preferred_element_type=F32)


def exact(a, b, dims=NN):
    return dot(a, b, dims, lax.Precision.HIGHEST)


def thirds(v):
    a = v.astype(BF16).astype(F32)
    b = (v - a).astype(BF16).astype(F32)
    return a, b, v - a - b


def stack3(v, rows):
    return jnp.concatenate([t.astype(BF16) for t in thirds(v)], axis=0)


def kernel(
    cot_ref, act_ref, logit_ref, saved_ref, w_ref, rw_ref, choice_ref,
    hid_ref, tok_ref, rg_ref,
    cot_out, act_out, p_out, cot_own, cot_pair, act_own, p_own, p_pair,
    hot_own, hot_pair, xbuf, w_self, w_other, acc_self, acc_other, part_in,
    gate_xy, gate_quarter, s_out, s_in, r_out, r_in, f_out, f_in,
    w_sem, w_send, w_recv, z_send, cot_recv, act_recv, p_recv, pair_send, pair_recv,
    x_send, x_one, x_two, core_send, core_recv, g_send, g_recv, q_send, q_recv,
    s_send, s_recv, r_send, r_recv, f_send, f_recv,
):
    me, xy = lax.axis_index("expert"), lax.axis_index("tensor")
    groups = lax.axis_size("expert")
    chips = groups // 2
    experts, cap = choice_ref.shape
    z, h = me // 2, me % 2
    e = z // 2
    x, y = xy // SIDE, xy % SIDE
    own_tokens = cot_ref.shape[0]
    other_core = z * 2 + (1 - h)
    pair_z = z + 1 - 2 * (z % 2)
    quarter = (z % 2) * 2 + h
    quarters = (other_core, pair_z * 2 + h, pair_z * 2 + (1 - h))

    def remote(src, dst, send, recv, expert_at, tensor_at):
        return pltpu.make_async_remote_copy(
            src_ref=src, dst_ref=dst, send_sem=send, recv_sem=recv,
            device_id=(expert_at, tensor_at), device_id_type=MESH,
        )

    def wait_bytes(ref, sem):
        pltpu.make_async_copy(ref, ref, sem).wait()

    def at_xy(i, j):
        return ((x + i) % SIDE) * SIDE + (y + j) % SIDE

    others_xy = [(i, j) for i in range(SIDE) for j in range(SIDE) if i or j]

    blocks = w_self.shape[0]
    for b in range(blocks):
        pltpu.make_async_copy(
            w_ref.at[:, pl.ds(pl.multiple_of(b * 2 * LANES + h * LANES, LANES), LANES)],
            w_self.at[b], w_sem,
        ).start()

    barrier = pltpu.get_barrier_semaphore()

    def greet(expert_at, tensor_at):
        pl.semaphore_signal(barrier, inc=1, device_id=(expert_at, tensor_at), device_id_type=MESH)

    def greet_column(k, carry):
        to = (z + 2 * k) % chips
        greet(to * 2, xy)
        greet(to * 2 + 1, xy)
        return carry

    lax.fori_loop(1, chips // 2, greet_column, 0)
    for q in quarters:
        greet(q, xy)
    for i, j in others_xy:
        greet(me, at_xy(i, j))

    tokens_at = iota((own_tokens, cap), 0) + me * own_tokens
    lane_expert = iota((own_tokens, LANES), 1)
    chosen = jnp.zeros((own_tokens, LANES), F32)
    for n in range(experts):
        hit = (choice_ref[n : n + 1, :] == tokens_at).astype(F32)
        chosen = jnp.where(lane_expert == n, jnp.sum(hit, axis=1, keepdims=True), chosen)
    before = (iota((own_tokens, own_tokens), 1) < iota((own_tokens, own_tokens), 0)).astype(BF16)
    place = dot(before, chosen.astype(BF16))
    wide = experts * SLOTS
    spread = (iota((LANES, wide), 1) // SLOTS == iota((LANES, wide), 0)).astype(BF16)
    chosen_wide = dot(chosen.astype(BF16), spread)
    place_wide = dot(place.astype(BF16), spread)
    slot_lane = (iota((own_tokens, wide), 1) % SLOTS).astype(F32)
    pick = jnp.where((chosen_wide > 0.5) & (place_wide == slot_lane), 1.0, 0.0)
    pick_bf = pick.astype(BF16)
    logits = logit_ref[...]
    grown = jnp.exp(logits - jnp.max(logits, axis=1, keepdims=True))
    probs = grown / jnp.sum(grown, axis=1, keepdims=True)
    copies = (iota((experts, LANES), 1) % experts == iota((experts, LANES), 0)).astype(F32)
    p_terms = thirds(exact(probs, copies))
    term = iota((own_tokens, LANES), 1) // experts
    p_wide = jnp.where(
        term == 0, p_terms[0], jnp.where(term == 1, p_terms[1], jnp.where(term == 2, p_terms[2], 0.0))
    )
    cot_slots = dot(pick_bf, cot_ref[...], TN).astype(BF16)
    cot_out[0] = cot_slots[:, :LANES]
    cot_out[1] = cot_slots[:, LANES:]
    act_slots = dot(pick_bf, act_ref[...], TN).astype(BF16)
    act_out[0] = act_slots[:, :LANES]
    act_out[1] = act_slots[:, LANES:]
    p_out[...] = dot(pick_bf, p_wide.astype(BF16), TN).astype(BF16)

    pl.semaphore_wait(barrier, (chips // 2 - 1) * 2 + len(quarters) + len(others_xy))

    row = pl.multiple_of(e * 2 * SLOTS + h * SLOTS, SLOTS)

    def dispatch(out, into, recv):
        def one(k):
            to = (z + 2 * k) % chips
            rows = pl.ds(pl.multiple_of((to // 2) * SLOTS, SLOTS), SLOTS)
            for c in range(2):
                remote(
                    out(c).at[rows], into.at[pl.ds(row, SLOTS)], z_send, recv, to * 2 + c, xy
                ).start()

        far = chips // 4
        one(far)

        def near(j, carry):
            one(far - j)
            one(far + j)
            return carry

        lax.fori_loop(1, far, near, 0)
        mine = pl.ds(pl.multiple_of(e * SLOTS, SLOTS), SLOTS)
        remote(out(1 - h).at[mine], into.at[pl.ds(row, SLOTS)], z_send, recv, other_core, xy).start()
        pltpu.make_async_copy(out(h).at[mine], into.at[pl.ds(row, SLOTS)], recv).start()

    dispatch(lambda c: cot_out.at[c], cot_own, cot_recv)

    for b in range(blocks):
        remote(
            w_ref.at[:, pl.ds(pl.multiple_of(b * 2 * LANES + (1 - h) * LANES, LANES), LANES)],
            w_other.at[b], w_send, w_recv, other_core, xy,
        ).start()

    wanted = choice_ref[pl.ds(e, 1), :].astype(F32)
    wanted_row = jnp.broadcast_to(wanted, (LANES, cap))
    wanted_col = jnp.broadcast_to(jnp.transpose(wanted_row)[:, :1], (cap, cap)).astype(I32)
    wanted_row = jnp.broadcast_to(wanted, (cap, cap)).astype(I32)
    earlier = (wanted_row // own_tokens == wanted_col // own_tokens) & (wanted_row < wanted_col)
    rank = jnp.sum(earlier.astype(F32), axis=1, keepdims=True).astype(I32)
    owner = wanted_col // own_tokens
    slot = (owner // 4) * (2 * SLOTS) + (owner % 2) * SLOTS + rank
    same = slot == iota((cap, cap), 1)
    parity = (owner // 2) % 2
    hot_own[...] = (same & (parity == z % 2)).astype(BF16)
    hot_pair[...] = (same & (parity != z % 2)).astype(BF16)

    wait_bytes(cot_own, cot_recv)
    to_pair = remote(cot_own, cot_pair, pair_send.at[0], pair_recv.at[0], pair_z * 2 + h, xy)
    to_pair.start()
    picked = dot(hot_own[...], cot_own[...])
    to_pair.wait_recv()
    xbuf[xy] = (picked + dot(hot_pair[...], cot_pair[...])).astype(BF16)

    half = cap // 2
    order = (1, 3, 2)
    one_step = []

    def rows_of(first):
        return pl.ds(first * half, half)

    def along(first, i, j):
        return at_xy(i, j) if first == 0 else at_xy(j, i)

    def send_block(first, block, recv, i, j):
        ref = xbuf.at[block, rows_of(first)]
        copy = remote(ref, ref, x_send, recv, me, along(first, i, j))
        copy.start()
        return copy

    for i in order:
        for first in range(2):
            send_block(first, xy, x_one.at[first, i], i, 0)
    for j in order:
        for first in range(2):
            send_block(first, xy, x_two.at[first, 0, j], 0, j)

    dispatch(lambda c: act_out.at[c], act_own, act_recv)
    dispatch(lambda c: p_out, p_own, p_recv)

    for i in order:
        for first in range(2):
            block = along(first, -i, 0)
            wait_bytes(xbuf.at[block, rows_of(first)], x_one.at[first, i])
            for j in order:
                send_block(first, block, x_two.at[first, i, j], 0, j)

    wait_bytes(w_self, w_sem)
    wait_bytes(w_other, w_recv)

    def product(first, blocks_at, weights):
        lhs = jnp.concatenate([xbuf[b, first * half : (first + 1) * half, :] for b in blocks_at], axis=1)
        rhs = jnp.concatenate([weights[b] for b in blocks_at], axis=1)
        return dot(lhs, rhs, NT)

    def span(first):
        return slice(first * half, (first + 1) * half)

    for first in range(2):
        at = [along(first, -i, 0) for i in range(SIDE)]
        acc_other[span(first), :] = product(first, at, w_other)
        acc_self[span(first), :] = product(first, at, w_self)
    for j in order:
        last = j == order[-1]
        for first in range(2):
            at = [along(first, -i, -j) for i in range(SIDE)]
            for i in range(SIDE):
                wait_bytes(xbuf.at[at[i], rows_of(first)], x_two.at[first, i, j])
            acc_other[span(first), :] += product(first, at, w_other)
            if last:
                remote(
                    acc_other.at[rows_of(first)], part_in.at[rows_of(first)], core_send, core_recv.at[first],
                    other_core, xy,
                ).start()
            else:
                acc_self[span(first), :] += product(first, at, w_self)
    for first in range(2):
        at = [along(first, -i, -order[-1]) for i in range(SIDE)]
        acc_self[span(first), :] += product(first, at, w_self)
    for first in range(2):
        wait_bytes(part_in.at[rows_of(first)], core_recv.at[first])
    pre = acc_self[...] + part_in[...]
    acc_self[...] = pre

    gate = exact(jnp.ones((8, saved_ref.shape[1]), F32), saved_ref[...].astype(F32) * pre, NT)
    pieces = cap // LANES
    for k in range(pieces):
        gate_xy[xy, k : k + 1, :] = gate[0:1, k * LANES : (k + 1) * LANES]
    for i, j in others_xy:
        remote(gate_xy.at[xy], gate_xy.at[xy], g_send, g_recv, me, at_xy(i, j)).start()

    wait_bytes(p_own, p_recv)
    p_to_pair = remote(p_own, p_pair, pair_send.at[1], pair_recv.at[1], pair_z * 2 + h, xy)
    p_to_pair.start()
    select = (iota((experts, LANES), 1) % experts == iota((experts, LANES), 0)) & (
        iota((experts, LANES), 1) < 3 * experts
    )
    p_slot = dot(select.astype(BF16), p_own[...], NT)
    mine = iota((experts, cap), 0) == e
    p_mine = jnp.sum(jnp.where(mine, p_slot, 0.0), axis=0, keepdims=True)
    slope = p_mine * (jnp.where(mine, 1.0, 0.0) - p_slot)
    wait_bytes(act_own, act_recv)

    wait_bytes(gate_xy.at[pl.ds(0, len(others_xy))], g_recv)
    gate_quarter[quarter] = jnp.sum(gate_xy[...], axis=0)
    for q in quarters:
        remote(gate_quarter.at[quarter], gate_quarter.at[quarter], q_send, q_recv, q, xy).start()
    wait_bytes(gate_quarter.at[pl.ds(0, len(quarters))], q_recv)
    total = jnp.sum(gate_quarter[...], axis=0)
    total_row = jnp.concatenate([total[k : k + 1, :] for k in range(pieces)], axis=1)
    rows3 = jnp.concatenate([total_row, jnp.zeros((7, cap), F32)], axis=0)
    s_three = dot(jnp.concatenate(thirds(rows3), axis=0).astype(BF16), hot_own[...])
    s_slot = s_three[0:1] + s_three[8:9] + s_three[16:17]

    slot_at = iota((experts, cap), 1)
    of_owner = (slot_at // (2 * SLOTS) == iota((experts, cap), 0)) & ((slot_at // SLOTS) % 2 == h)
    fold = (iota((cap, LANES), 0) % SLOTS == iota((cap, LANES), 1)).astype(F32)
    s_rows = exact(jnp.where(of_owner, s_slot, 0.0), fold)
    for k in range(experts):
        s_out[k] = s_rows[k : k + 1, :]
    w_slot = s_slot * slope
    r_three = dot(jnp.concatenate(thirds(w_slot), axis=0).astype(BF16), act_own[...])
    r_part = r_three[:experts] + r_three[experts : 2 * experts] + r_three[2 * experts :]
    r_out[...] = r_part.astype(BF16)

    def back(out, into, send, recv):
        def one(k):
            to = (z + 2 * k) % chips
            remote(out(to // 2), into.at[e], send, recv, to * 2 + h, xy).start()

        far = chips // 4
        one(far)

        def near(j, carry):
            one(far - j)
            one(far + j)
            return carry

        lax.fori_loop(1, far, near, 0)

    back(lambda k: s_out.at[k], s_in, s_send, s_recv)
    back(lambda k: r_out, r_in, r_send, r_recv)
    s_in[e] = s_out[e]
    r_in[e] = r_out[...]

    p_to_pair.wait_recv()
    gates = dot(hot_own[...], p_own[...]) + dot(hot_pair[...], p_pair[...])
    gate_col = jnp.sum(jnp.where(iota((cap, LANES), 1) == e, gates, 0.0), axis=1, keepdims=True)
    hid_ref[...] = (gate_col * acc_self[...]).astype(BF16)

    wait_bytes(s_in.at[pl.ds(0, experts - 1)], s_recv)
    s_all = jnp.concatenate([s_in[k] for k in range(experts)], axis=0)
    unfold = (iota((LANES, wide), 1) % SLOTS == iota((LANES, wide), 0)).astype(F32)
    own_lane = iota((experts, wide), 1) // SLOTS == iota((experts, wide), 0)
    s_wide = jnp.where(own_lane, exact(s_all, unfold), 0.0)
    score = exact(pick, s_wide, NT)
    inner = jnp.sum(probs * score, axis=1, keepdims=True)
    logit_grad = (probs * (score - inner)).astype(BF16)
    tok_ref[...] = dot(logit_grad, rw_ref[...], NT).astype(BF16)

    wait_bytes(r_in.at[pl.ds(0, experts - 1)], r_recv)
    f_out[...] = jnp.sum(r_in[...].astype(F32), axis=0)
    f_in[quarter] = f_out[...]
    for q in quarters:
        remote(f_out, f_in.at[quarter], f_send, f_recv, q, xy).start()
    wait_bytes(f_in.at[pl.ds(0, len(quarters))], f_recv)
    left = f_in[0] + f_in[2]
    right = f_in[1] + f_in[3]
    both = jnp.concatenate([left, right], axis=1)
    both = jnp.concatenate([both, jnp.zeros((LANES - experts, both.shape[1]), F32)], axis=0)
    rg_ref[...] = jnp.transpose(both)[:, :experts]

    for ref in (w_other, part_in):
        pass
    wait_bytes(w_other, w_send)
    def sent(ref):
        pltpu.make_async_copy(ref, ref, z_send).wait()

    for ref in (cot_own, act_own, p_own):
        sent(ref.at[pl.ds(0, cap - SLOTS)])
    to_pair.wait_send()
    p_to_pair.wait_send()
    for _ in range(15):
        wait_bytes(xbuf.at[0], x_send)
    wait_bytes(acc_other, core_send)
    wait_bytes(gate_xy.at[pl.ds(0, len(others_xy))], g_send)
    wait_bytes(gate_quarter.at[pl.ds(0, len(quarters))], q_send)
    wait_bytes(s_in.at[pl.ds(0, experts - 1)], s_send)
    wait_bytes(r_in.at[pl.ds(0, experts - 1)], r_send)
    wait_bytes(f_in.at[pl.ds(0, len(quarters))], f_send)


def on_device(
    cotangent, activations, router_logits, saved_hidden, down_weight, router_weight, choices
):
    experts, cap = choices.shape
    own_tokens, feats = cotangent.shape
    hidden = down_weight.shape[0]
    wide = experts * SLOTS
    blocks = SIDE * SIDE
    vmem = pl.BlockSpec(memory_space=pltpu.VMEM)
    dma = pltpu.SemaphoreType.DMA
    return pl.pallas_call(
        kernel,
        out_shape=(
            jax.ShapeDtypeStruct((cap, hidden), BF16),
            jax.ShapeDtypeStruct((own_tokens, feats), BF16),
            jax.ShapeDtypeStruct((feats, experts), F32),
        ),
        in_specs=[vmem, vmem, vmem, vmem, pl.BlockSpec(memory_space=pl.ANY), vmem, vmem],
        out_specs=(vmem, vmem, vmem),
        scratch_shapes=[
            pltpu.VMEM((2, wide, LANES), BF16),
            pltpu.VMEM((2, wide, LANES), BF16),
            pltpu.VMEM((wide, LANES), BF16),
            pltpu.VMEM((cap, LANES), BF16),
            pltpu.VMEM((cap, LANES), BF16),
            pltpu.VMEM((cap, LANES), BF16),
            pltpu.VMEM((cap, LANES), BF16),
            pltpu.VMEM((cap, LANES), BF16),
            pltpu.VMEM((cap, cap), BF16),
            pltpu.VMEM((cap, cap), BF16),
            pltpu.VMEM((blocks, cap, LANES), BF16),
            pltpu.VMEM((blocks, hidden, LANES), BF16),
            pltpu.VMEM((blocks, hidden, LANES), BF16),
            pltpu.VMEM((cap, hidden), F32),
            pltpu.VMEM((cap, hidden), F32),
            pltpu.VMEM((cap, hidden), F32),
            pltpu.VMEM((blocks, cap // LANES, LANES), F32),
            pltpu.VMEM((4, cap // LANES, LANES), F32),
            pltpu.VMEM((experts, 1, LANES), F32),
            pltpu.VMEM((experts, 1, LANES), F32),
            pltpu.VMEM((experts, LANES), BF16),
            pltpu.VMEM((experts, experts, LANES), BF16),
            pltpu.VMEM((experts, LANES), F32),
            pltpu.VMEM((4, experts, LANES), F32),
            dma(()), dma(()), dma(()),
            dma(()), dma(()), dma(()), dma(()),
            dma((2,)), dma((2,)),
            dma(()), dma((2, SIDE)), dma((2, SIDE, SIDE)),
            dma(()), dma((2,)),
            dma(()), dma(()), dma(()), dma(()),
            dma(()), dma(()), dma(()), dma(()), dma(()), dma(()),
        ],
        compiler_params=pltpu.CompilerParams(
            collective_id=0, has_side_effects=True, vmem_limit_bytes=48 * 2**20
        ),
        cost_estimate=pl.CostEstimate(
            flops=2 * cap * hidden * feats * blocks, bytes_accessed=4 * 2**20, transcendentals=0
        ),
        name="gated_moe_backward",
    )(cotangent, activations, router_logits, saved_hidden, down_weight, router_weight, choices)


def solution(mesh):
    placed = (
        P("expert", "tensor"),
        P("expert", "tensor"),
        P("expert", None),
        P(None, ("expert", "tensor")),
        P(("expert", "tensor"), None),
        P("tensor", None),
        P(),
    )
    return jax.shard_map(
        on_device,
        mesh=mesh,
        in_specs=placed,
        out_specs=(P(None, ("expert", "tensor")), P("expert", "tensor"), P("tensor", None)),
        check_vma=False,
    )
```

time: 589 us -> 110 us (0.19)
  blocking collectives: 329 us -> 0 us
  waiting for transfers between devices: 170 us -> 0 us
  Pallas kernels: 0 us -> 100 us
  other arithmetic: 62.9 us -> 0 us
  between operations: 14.3 us -> 0.65 us
    psum x2 -> x0, blocking collectives: 207 us -> none  [the longest x1 177 us: on_device(): router_grad = lax.psum(router_part, 'expert')]
    all_gather x2 -> x0, waiting for transfers between devices: 169 us -> none  [the longest x1 146 us: on_device(): block_rows = lax.all_gather(cotangent, 'expert', axis=0, tiled=True)]
    all_gather x2 -> x0, blocking collectives: 122 us -> none  [the longest x1 67.1 us: on_device(): all_parts = lax.all_gather(gate_part[None, :], 'expert', axis=0, tiled=True)]
    pallas_call x0 -> x1, Pallas kernels: none -> 100 us  [on_device(): pl.pallas_call(kernel, out_shape=(jax.ShapeDtypeStruct((cap, hidden), BF1...]
    unnamed x6 -> x0, other arithmetic: 58.5 us -> none
  transfers between devices with their start and end apart: 2 -> 0, of which waited for: 2 -> 0; matrix products, arithmetic and copies ran while one was open for 1% -> 0% of each run, Pallas kernels for 0% -> 0%
where the time goes in v1:
time: 110 us; the launch traced here: 109 us
  Pallas kernels  100 us (91%)
  local copies, waits for them, and re-layouts  8.4 us (8%)
    pallas_call x1, Pallas kernels, on_device(): pl.pallas_call(kernel, out_shape=(jax.ShapeDtypeStruct((cap, hidden), BF1...  100 us
    unnamed x14, local copies, waits for them, and re-layouts  7.72 us

profile of v1, /device:TPU:1, one launch (start us, length us, event | category | flops | bytes accessed | tf_op | source)
XLA Modules:
  0.0 109.5 jit_solution(14191516733208460023)
XLA Ops:
  0.6 0.8 copy.10.logit_ref
  1.4 0.8 copy.11.rw_ref
  2.2 0.0 copy-start
  2.2 1.6 %copy-done = bf16[256,4096]{1,0:T(8,128)(2,1)S(1)} copy-done((bf16[256,4096]{1,0:T(8,128)(2,1)S(1)}, bf16[256,4096]{1,0:T(8,128)(2,1)}, u32[]{:S(2)}) %copy-start) | copy-done | bytes 2097176
  3.8 0.0 copy-start.1
  3.8 0.9 copy-done.1
  4.8 0.0 copy-start.2
  4.8 0.8 copy-done.2
  5.5 0.0 copy-start.3
  5.5 0.8 copy-done.3
  6.3 0.0 copy-start.4
  6.3 0.8 copy-done.4
  7.0 100.4 %gated_moe_backward.1 = (bf16[512,256]{1,0:T(8,128)(2,1)S(1)}, bf16[64,256]{1,0:T(8,128)(2,1)S(1)}, f32[256,16]{1,0:T(8,128)S(1)}) custom-call(bf16[64,256]{1,0:T(8,128)(2,1)S(1)} %copy-done.2, bf16[64,256]{1,0:T(8,128)(2,1)S(1)} %copy-done.3, f32[64,16]{1,0:T(8,128)S(1)} %copy.10.logit_ref, bf16[512,256]{1,0:T(8,128)(2,1)S(1)} %copy-done.1, ...), custom_call_target="tpu_custom_call" | custom-call | flops 1073741824 | bytes 4194304 | tf_op jit(solution)/shard_map/gated_moe_backward/pallas_call | solution.py:379
  107.5 0.7 copy.12
  108.1 0.7 copy.15
  108.8 0.6 copy.16
Async XLA Ops:
  2.2 1.6 %copy-start = (bf16[256,4096]{1,0:T(8,128)(2,1)S(1)}, bf16[256,4096]{1,0:T(8,128)(2,1)}, u32[]{:S(2)}) copy-start(bf16[256,4096]{1,0:T(8,128)(2,1)} %w_ref.1) | copy-start | bytes 6291460
  3.8 0.9 copy-start.1
  4.8 0.8 copy-start.2
  5.5 0.8 copy-start.3
  6.3 0.8 copy-start.4

commit v2 on v1

v2 whole, which is shorter than its diff:
```python
import functools

import jax
import jax.numpy as jnp
from jax import lax
from jax.experimental import pallas as pl
from jax.experimental.pallas import tpu as pltpu
from jax.sharding import PartitionSpec as P

MESH = pl.DeviceIdType.MESH
F32 = jnp.float32
BF16 = jnp.bfloat16
I32 = jnp.int32
SLOTS = 16
SIDE = 4
LANES = 128
NT = (((1,), (1,)), ((), ()))
TN = (((0,), (0,)), ((), ()))
NN = (((1,), (0,)), ((), ()))


def iota(shape, axis):
    return lax.broadcasted_iota(I32, shape, axis)


def dot(a, b, dims=NN, precision=None):
    return lax.dot_general(a, b, dims, precision=precision, preferred_element_type=F32)


def exact(a, b, dims=NN):
    return dot(a, b, dims, lax.Precision.HIGHEST)


def thirds(v):
    a = v.astype(BF16).astype(F32)
    b = (v - a).astype(BF16).astype(F32)
    return a, b, v - a - b


def shift_of(n):
    return n.bit_length() - 1


def kernel(
    cot_hbm, act_hbm, logit_hbm, saved_hbm, w_hbm, rw_hbm, choice_hbm,
    hid_ref, tok_ref, rg_ref,
    cot_ref, act_ref, logit_ref, saved_ref, saved_other, rw_ref, choice_ref,
    cot_out, act_out, p_out, up, down, cot_own, cot_pair, act_own, p_own, p_pair,
    hot_own, hot_pair, xbuf, w_self, w_other, acc_self, acc_other, part_in,
    gate_one, gate_two, s_out, s_in, r_out, r_in, f_out, f_in,
    in_sem, w_sem, w_send, w_recv, saved_send, saved_recv,
    up_send, up_recv, near_send, hop_send, cot_recv, pair_send, pair_recv,
    act_send, act_recv, p_send, p_recv, p_two_send, p_two_recv, p_pair_send, p_pair_recv,
    x_send, x_one, x_two, core_send, core_recv, one_send, one_recv, two_send, two_recv,
    s_send, s_recv, r_send, r_recv, f_send, f_recv,
):
    me, xy = lax.axis_index("expert"), lax.axis_index("tensor")
    groups = lax.axis_size("expert")
    chips = groups // 2
    experts, cap = choice_ref.shape
    own_tokens, feats = cot_ref.shape
    z, h = me // 2, me % 2
    e = z // 2
    x, y = xy // SIDE, xy % SIDE
    other_core = z * 2 + (1 - h)
    pair_z = z + 1 - 2 * (z % 2)
    pair = pair_z * 2 + h
    quarter = (z % 2) * 2 + h
    quarters = (other_core, pair, pair_z * 2 + (1 - h))
    far = 4
    token_shift, slot_shift = shift_of(own_tokens), shift_of(SLOTS)

    def remote(src, dst, send, recv, expert_at, tensor_at=xy):
        return pltpu.make_async_remote_copy(
            src_ref=src, dst_ref=dst, send_sem=send, recv_sem=recv,
            device_id=(expert_at, tensor_at), device_id_type=MESH,
        )

    def wait_bytes(ref, sem):
        pltpu.make_async_copy(ref, ref, sem).wait()

    waits = {}

    def later(name, ref, sem):
        waits[name] = lambda: wait_bytes(ref, sem)

    def finish(name):
        waits.pop(name)()

    def at_xy(i, j):
        return ((x + i) % SIDE) * SIDE + (y + j) % SIDE

    def at_z(k):
        return (z + 2 * k + 2 * chips) % chips

    arrays = {
        "choice": (choice_hbm, choice_ref), "cot": (cot_hbm, cot_ref), "act": (act_hbm, act_ref),
        "logit": (logit_hbm, logit_ref), "saved": (saved_hbm, saved_ref), "rw": (rw_hbm, rw_ref),
    }

    def load(*names):
        for name in names:
            src, dst = arrays[name]
            sem = in_sem.at[list(arrays).index(name)]
            pltpu.make_async_copy(src, dst, sem).start()
            later(name, dst, sem)

    load("choice", "cot")

    barrier = pltpu.get_barrier_semaphore()

    def greet(expert_at, tensor_at):
        pl.semaphore_signal(barrier, inc=1, device_id=(expert_at, tensor_at), device_id_type=MESH)

    near_steps = [k * sign for k in range(far, 0, -1) for sign in (1, -1)]
    for k in near_steps:
        for c in range(2):
            greet(at_z(k) * 2 + c, xy)
    for i in range(1, SIDE):
        greet(me, at_xy(0, i))
        greet(me, at_xy(i, 0))
        for q in quarters:
            greet(q, at_xy(i, 0))
    for q in quarters:
        greet(q, xy)
    greeted = 2 * len(near_steps) + 5 * (SIDE - 1) + len(quarters)

    finish("choice")
    tokens_at = iota((own_tokens, cap), 0) + me * own_tokens
    lane_expert = iota((own_tokens, LANES), 1)
    chosen = jnp.zeros((own_tokens, LANES), F32)
    for n in range(experts):
        hit = jnp.where(choice_ref[n : n + 1, :] == tokens_at, 1.0, 0.0)
        chosen = jnp.where(lane_expert == n, jnp.sum(hit, axis=1, keepdims=True), chosen)
    before = (iota((own_tokens, own_tokens), 1) < iota((own_tokens, own_tokens), 0)).astype(F32).astype(BF16)
    place = dot(before, chosen.astype(BF16))
    wide = experts * SLOTS
    group_of = (jnp.right_shift(iota((LANES, wide), 1), slot_shift) + e) & (experts - 1)
    spread = (group_of == iota((LANES, wide), 0)).astype(F32).astype(BF16)
    chosen_wide = dot(chosen.astype(BF16), spread)
    place_wide = dot(place.astype(BF16), spread)
    slot_lane = (iota((own_tokens, wide), 1) & (SLOTS - 1)).astype(F32)
    pick = jnp.where((chosen_wide > 0.5) & (place_wide == slot_lane), 1.0, 0.0)
    pick_bf = pick.astype(BF16)
    finish("cot")
    cot_slots = dot(pick_bf, cot_ref[...], TN).astype(BF16)
    cot_out[0] = cot_slots[:, :LANES].reshape(experts, SLOTS, LANES)
    cot_out[1] = cot_slots[:, LANES:].reshape(experts, SLOTS, LANES)

    pl.semaphore_wait(barrier, greeted)

    slots_of_core = pl.ds(pl.multiple_of(h * SLOTS, SLOTS), SLOTS)
    for c in range(2):
        remote(
            cot_out.at[c, pl.ds(far + 1, far - c)], up.at[pl.ds(0, far - c), slots_of_core], up_send.at[0],
            up_recv.at[0], at_z(far) * 2 + c,
        ).start()
        remote(
            cot_out.at[c, pl.ds(2 * far + 1 - c, far - 1 + c)], down.at[pl.ds(1 - c, far - 1 + c), slots_of_core],
            up_send.at[1], up_recv.at[1], at_z(-far) * 2 + c,
        ).start()
    pair_rows = 2 * SLOTS

    def rows_from(k):
        return pl.ds(pl.multiple_of(((e - k + experts) % experts) * pair_rows, pair_rows), pair_rows)

    mine = pl.ds(pl.multiple_of(e * pair_rows + h * SLOTS, SLOTS), SLOTS)
    for k in near_steps:
        for c in range(2):
            remote(
                cot_out.at[c, k % experts], cot_own.at[mine], near_send, cot_recv.at[k % experts], at_z(k) * 2 + c
            ).start()
    remote(cot_out.at[1 - h, 0], cot_own.at[mine], near_send, cot_recv.at[0], other_core).start()
    pltpu.make_async_copy(cot_out.at[h, 0], cot_own.at[mine], cot_recv.at[0]).start()
    load("act", "logit")
    later("near", cot_own.at[pl.ds(0, (2 * len(near_steps) + 1) * SLOTS)], near_send)

    blocks = w_self.shape[0]
    for b in range(blocks):
        pltpu.make_async_copy(
            w_hbm.at[:, pl.ds(pl.multiple_of(b * 2 * LANES + h * LANES, LANES), LANES)],
            w_self.at[b], w_sem,
        ).start()
    later("w", w_self, w_sem)

    load("saved", "rw")

    finish("act")
    act_slots = dot(pick_bf, act_ref[...], TN).astype(BF16)
    act_out[0] = act_slots[:, :LANES].reshape(experts, SLOTS, LANES)
    act_out[1] = act_slots[:, LANES:].reshape(experts, SLOTS, LANES)
    finish("logit")
    logits = logit_ref[...]
    grown = jnp.exp(logits - jnp.max(logits, axis=0, keepdims=True))
    probs = grown / jnp.sum(grown, axis=0, keepdims=True)
    lane = iota((experts, LANES), 1)
    copies = jnp.where((lane & (experts - 1)) == iota((experts, LANES), 0), 1.0, 0.0)
    p_terms = thirds(exact(probs, copies, TN))
    term = jnp.right_shift(iota((own_tokens, LANES), 1), shift_of(experts))
    p_wide = jnp.where(
        term == 0, p_terms[0], jnp.where(term == 1, p_terms[1], jnp.where(term == 2, p_terms[2], 0.0))
    )
    p_out[...] = dot(pick_bf, p_wide.astype(BF16), TN).astype(BF16).reshape(experts, SLOTS, LANES)

    middle = experts // 2

    def act_to(k):
        for c in range(2):
            remote(act_out.at[c, k], act_own.at[mine], act_send, act_recv, at_z(k) * 2 + c).start()

    def act_each(j, carry):
        act_to(middle - j)
        act_to(middle + j)
        return carry

    def p_to(k):
        for c in range(2):
            remote(p_out.at[k], p_own.at[mine], p_send, p_recv, at_z(k) * 2 + c).start()

    def send_rest():
        for m in range(SIDE - 1, 0, -1):
            p_to(m * SIDE + y)

        @pl.when(y != 0)
        def _():
            p_to(y)

        @pl.when(y == 0)
        def _():
            remote(p_out.at[0], p_own.at[mine], p_send, p_recv, other_core).start()
            pltpu.make_async_copy(p_out.at[0], p_own.at[mine], p_recv).start()

        act_to(middle)
        lax.fori_loop(1, middle, act_each, 0)
        remote(act_out.at[1 - h, 0], act_own.at[mine], act_send, act_recv, other_core).start()
        pltpu.make_async_copy(act_out.at[h, 0], act_own.at[mine], act_recv).start()
        later("act_send", act_own.at[pl.ds(0, cap - SLOTS)], act_send)
        later("act_slots", act_own, act_recv)
        waits["p_send"] = p_sent

    def p_sent():
        sends = 2 * experts // SIDE

        @pl.when(y == 0)
        def _():
            wait_bytes(p_own.at[pl.ds(0, (sends - 1) * SLOTS)], p_send)

        @pl.when(y != 0)
        def _():
            wait_bytes(p_own.at[pl.ds(0, sends * SLOTS)], p_send)

    def share_p():
        wait_bytes(p_own.at[pl.ds(0, cap // SIDE)], p_recv)
        for m in range(SIDE):
            rows = rows_from(m * SIDE + y)
            for j in (2, 1, 3):
                remote(p_own.at[rows], p_own.at[rows], p_two_send, p_two_recv, me, at_xy(0, j)).start()
        rest = p_own.at[pl.ds(0, cap - cap // SIDE)]
        later("p_two_send", rest, p_two_send)
        later("p_slots", rest, p_two_recv)

    def share(k):
        rows = rows_from(k)
        wait_bytes(cot_own.at[rows], cot_recv.at[k % experts])
        remote(cot_own.at[rows], cot_pair.at[rows], pair_send, pair_recv, pair).start()

    later("pair_send", cot_pair, pair_send)
    later("pair", cot_pair, pair_recv)

    def hop_up(j):
        remote(
            up.at[j], cot_own.at[rows_from(far)], hop_send.at[0], cot_recv.at[far + 1 + j], at_z(1 + j) * 2 + h
        ).start()

    def hop_down(j):
        remote(
            down.at[j], cot_own.at[rows_from(-far)], hop_send.at[1], cot_recv.at[2 * far + j], at_z(j - far) * 2 + h
        ).start()

    for k in (0, 1, -1, 2, -2):
        share(k)
    most, fewer = pl.ds(0, far), pl.ds(0, far - 1)

    @pl.when(h == 0)
    def _():
        wait_bytes(up.at[most], up_recv.at[0])
        hop_up(far - 1)

    @pl.when(h == 1)
    def _():
        wait_bytes(up.at[fewer], up_recv.at[0])

    for j in range(far - 2, -1, -1):
        hop_up(j)

    @pl.when(h == 1)
    def _():
        wait_bytes(down.at[most], up_recv.at[1])
        hop_down(0)

    @pl.when(h == 0)
    def _():
        wait_bytes(down.at[fewer], up_recv.at[1])

    for j in range(1, far):
        hop_down(j)

    def hopped():
        @pl.when(h == 0)
        def _():
            wait_bytes(up.at[most], hop_send.at[0])
            wait_bytes(down.at[fewer], hop_send.at[1])

        @pl.when(h == 1)
        def _():
            wait_bytes(up.at[fewer], hop_send.at[0])
            wait_bytes(down.at[most], hop_send.at[1])

    waits["hop"] = hopped
    relayed = cot_own.at[pl.ds(0, (2 * far - 1) * SLOTS)]
    later("up_send", relayed, up_send.at[0])
    later("down_send", relayed, up_send.at[1])

    wanted = choice_ref[pl.ds(e, 1), :].astype(F32)
    wanted_col = jnp.transpose(jnp.broadcast_to(wanted, (LANES, cap)))[:, :1].astype(I32)
    wanted_row = wanted.astype(I32)
    owner_col = jnp.right_shift(wanted_col, token_shift)
    owner_row = jnp.right_shift(wanted_row, token_shift)
    earlier = (owner_row == owner_col) & (wanted_row < wanted_col)
    rank = jnp.sum(jnp.where(earlier, 1.0, 0.0), axis=1, keepdims=True).astype(I32)
    slot = jnp.right_shift(owner_col, 2) * pair_rows + (owner_col & 1) * SLOTS + rank
    ours = (jnp.right_shift(owner_col, 1) & 1) == z % 2
    slot_lanes = iota((cap, cap), 1)
    hot_own[...] = jnp.where(jnp.where(ours, slot, -1) == slot_lanes, 1.0, 0.0).astype(BF16)
    hot_pair[...] = jnp.where(jnp.where(ours, -1, slot) == slot_lanes, 1.0, 0.0).astype(BF16)

    for k in (3, -3, 4, -4, 5, -5, 6, -6, 7, -7, 8):
        share(k)
    picked = dot(hot_own[...], cot_own[...])
    finish("pair")
    xbuf[xy] = (picked + dot(hot_pair[...], cot_pair[...])).astype(BF16)

    half = cap // 2
    order = (1, 3, 2)

    def rows_of(first):
        return pl.ds(first * half, half)

    def along(first, i, j):
        return at_xy(i, j) if first == 0 else at_xy(j, i)

    def send_block(first, block, recv, i, j):
        ref = xbuf.at[block, rows_of(first)]
        remote(ref, ref, x_send, recv, me, along(first, i, j)).start()

    for i in order:
        for first in range(2):
            send_block(first, xy, x_one.at[first, i], i, 0)
    for j in order:
        for first in range(2):
            send_block(first, xy, x_two.at[first, 0, j], 0, j)
    for b in range(blocks):
        remote(
            w_hbm.at[:, pl.ds(pl.multiple_of(b * 2 * LANES + (1 - h) * LANES, LANES), LANES)],
            w_other.at[b], w_send, w_recv, other_core,
        ).start()
    later("w_send", w_other, w_send)
    later("w_other", w_other, w_recv)
    remote(saved_hbm, saved_other, saved_send, saved_recv, other_core).start()
    later("saved_send", saved_other, saved_send)
    later("saved_other", saved_other, saved_recv)

    later("x_send", xbuf.at[pl.ds(0, SIDE * SIDE - 1)], x_send)

    def relay(i):
        for first in range(2):
            block = along(first, -i, 0)
            wait_bytes(xbuf.at[block, rows_of(first)], x_one.at[first, i])
            for j in order:
                send_block(first, block, x_two.at[first, i, j], 0, j)

    send_rest()
    relay(1)
    relay(3)
    relay(2)
    share_p()

    finish("w")
    finish("w_other")

    def product(first, blocks_at, weights):
        lhs = jnp.concatenate([xbuf[b, first * half : (first + 1) * half, :] for b in blocks_at], axis=1)
        rhs = jnp.concatenate([weights[b] for b in blocks_at], axis=1)
        return dot(lhs, rhs, NT)

    def span(first):
        return slice(first * half, (first + 1) * half)

    for first in range(2):
        at = [along(first, -i, 0) for i in range(SIDE)]
        acc_other[span(first), :] = product(first, at, w_other)
        acc_self[span(first), :] = product(first, at, w_self)
    for j in order:
        for first in range(2):
            at = [along(first, -i, -j) for i in range(SIDE)]
            for i in range(SIDE):
                wait_bytes(xbuf.at[at[i], rows_of(first)], x_two.at[first, i, j])
            acc_other[span(first), :] += product(first, at, w_other)
            acc_self[span(first), :] += product(first, at, w_self)

    finish("saved")
    finish("saved_other")
    prod = saved_ref[...].astype(F32) * acc_self[...] + saved_other[...].astype(F32) * acc_other[...]
    gate = jnp.sum(jnp.transpose(prod[:, :LANES] + prod[:, LANES:]), axis=0, keepdims=True)
    pieces = cap // LANES
    slot_one = x * 4 + quarter
    for k in range(pieces):
        gate_one[slot_one, k : k + 1, :] = gate[0:1, k * LANES : (k + 1) * LANES]
    for i in (2, 1, 3, 0):
        for q in quarters + (() if i == 0 else (me,)):
            remote(gate_one.at[slot_one], gate_one.at[slot_one], one_send, one_recv, q, at_xy(i, 0)).start()
    later("one_send", gate_one.at[pl.ds(0, 4 * SIDE - 1)], one_send)
    wait_bytes(gate_one.at[pl.ds(0, 4 * SIDE - 1)], one_recv)
    gate_two[y] = jnp.sum(gate_one[...], axis=0)
    for j in (2, 1, 3):
        remote(gate_two.at[y], gate_two.at[y], two_send, two_recv, me, at_xy(0, j)).start()
    later("two_send", gate_two.at[pl.ds(0, SIDE - 1)], two_send)

    for first in range(2):
        remote(
            acc_other.at[rows_of(first)], part_in.at[rows_of(first)], core_send, core_recv, other_core
        ).start()
    later("core_send", acc_other, core_send)
    later("part", part_in, core_recv)

    finish("p_slots")
    p_to_pair = remote(p_own, p_pair, p_pair_send, p_pair_recv, pair)
    p_to_pair.start()
    later("p_pair_send", p_pair, p_pair_send)
    later("p_pair", p_pair, p_pair_recv)
    select = jnp.where(lane < 3 * experts, copies, 0.0)
    p_slot = dot(select.astype(BF16), p_own[...], NT)
    mine_row = iota((experts, cap), 0) == e
    p_mine = jnp.sum(jnp.where(mine_row, p_slot, 0.0), axis=0, keepdims=True)
    slope = p_mine * (jnp.where(mine_row, 1.0, 0.0) - p_slot)
    finish("act_slots")

    wait_bytes(gate_two.at[pl.ds(0, SIDE - 1)], two_recv)
    total = jnp.sum(gate_two[...], axis=0)
    total_row = jnp.concatenate([total[k : k + 1, :] for k in range(pieces)], axis=1)
    rows3 = jnp.concatenate([total_row, jnp.zeros((7, cap), F32)], axis=0)
    s_three = dot(jnp.concatenate(thirds(rows3), axis=0).astype(BF16), hot_own[...])
    s_slot = s_three[0:1] + s_three[8:9] + s_three[16:17]

    def back(name, out, into, send, recv):
        def one(k):
            to = (z + 2 * k) % chips
            remote(out(to // 2), into.at[e], send, recv, to * 2 + h).start()

        middle = experts // 2
        one(middle)

        def each(j, carry):
            one(middle - j)
            one(middle + j)
            return carry

        lax.fori_loop(1, middle, each, 0)
        later(name + "_send", into.at[pl.ds(0, experts - 1)], send)
        later(name, into.at[pl.ds(0, experts - 1)], recv)

    w_slot = s_slot * slope
    r_three = dot(jnp.concatenate(thirds(w_slot), axis=0).astype(BF16), act_own[...])
    r_part = r_three[:experts] + r_three[experts : 2 * experts] + r_three[2 * experts :]
    r_out[...] = r_part.astype(BF16)
    back("r", lambda k: r_out, r_in, r_send, r_recv)
    slot_at = iota((experts, cap), 1)
    of_owner = (jnp.right_shift(slot_at, slot_shift + 1) == iota((experts, cap), 0)) & (
        (jnp.right_shift(slot_at, slot_shift) & 1) == h
    )
    fold = jnp.where((iota((cap, LANES), 0) & (SLOTS - 1)) == iota((cap, LANES), 1), 1.0, 0.0)
    s_spread = jnp.concatenate(thirds(jnp.where(of_owner, s_slot, 0.0)), axis=0).astype(BF16)
    s_three = dot(s_spread, fold.astype(BF16))
    s_rows = s_three[:experts] + s_three[experts : 2 * experts] + s_three[2 * experts :]
    for k in range(experts):
        s_out[k] = s_rows[k : k + 1, :]

    back("s", lambda k: s_out.at[k], s_in, s_send, s_recv)
    r_in[e] = r_out[...]
    s_in[e] = s_out[e]

    finish("p_pair")
    gates = dot(hot_own[...], p_own[...]) + dot(hot_pair[...], p_pair[...])
    gate_col = jnp.sum(jnp.where(iota((cap, LANES), 1) == e, gates, 0.0), axis=1, keepdims=True)
    finish("part")
    hid_ref[...] = (gate_col * (acc_self[...] + part_in[...])).astype(BF16)

    finish("rw")
    finish("s")
    s_all = jnp.concatenate([s_in[k] for k in range(experts)], axis=0)
    unfold = jnp.where((iota((LANES, wide), 1) & (SLOTS - 1)) == iota((LANES, wide), 0), 1.0, 0.0)
    s_three = dot(jnp.concatenate(thirds(s_all), axis=0).astype(BF16), unfold.astype(BF16))
    s_sum = s_three[:experts] + s_three[experts : 2 * experts] + s_three[2 * experts :]
    own_lane = ((jnp.right_shift(iota((experts, wide), 1), slot_shift) + e) & (experts - 1)) == iota((experts, wide), 0)
    score3 = dot(jnp.concatenate(thirds(jnp.where(own_lane, s_sum, 0.0)), axis=0).astype(BF16), pick_bf, NT)
    score = score3[:experts] + score3[experts : 2 * experts] + score3[2 * experts :]
    inner = jnp.sum(probs * score, axis=0, keepdims=True)
    logit_grad = (probs * (score - inner)).astype(BF16)
    tok_ref[...] = dot(logit_grad, rw_ref[...], TN).astype(BF16)

    finish("r")
    f_out[...] = jnp.sum(r_in[...].astype(F32), axis=0)
    f_in[quarter] = f_out[...]
    for q in quarters:
        remote(f_out, f_in.at[quarter], f_send, f_recv, q).start()
    later("f_send", f_in.at[pl.ds(0, len(quarters))], f_send)
    wait_bytes(f_in.at[pl.ds(0, len(quarters))], f_recv)
    rg_ref[:, :LANES] = f_in[0] + f_in[2]
    rg_ref[:, LANES:] = f_in[1] + f_in[3]

    for name in list(waits):
        finish(name)


def on_device(
    cotangent, activations, router_logits, saved_hidden, down_weight, router_weight, choices
):
    experts, cap = choices.shape
    own_tokens, feats = cotangent.shape
    hidden = down_weight.shape[0]
    wide = experts * SLOTS
    blocks = SIDE * SIDE
    vmem = pl.BlockSpec(memory_space=pltpu.VMEM)
    hbm = pl.BlockSpec(memory_space=pltpu.HBM)
    dma = pltpu.SemaphoreType.DMA
    hidden_grad, token_grad, router_grad = pl.pallas_call(
        kernel,
        out_shape=(
            jax.ShapeDtypeStruct((cap, hidden), BF16),
            jax.ShapeDtypeStruct((own_tokens, feats), BF16),
            jax.ShapeDtypeStruct((experts, feats), F32),
        ),
        in_specs=[hbm] * 7,
        out_specs=(vmem, vmem, vmem),
        scratch_shapes=[
            pltpu.VMEM((own_tokens, feats), BF16),
            pltpu.VMEM((own_tokens, feats), BF16),
            pltpu.VMEM((experts, own_tokens), F32),
            pltpu.VMEM((cap, hidden), BF16),
            pltpu.VMEM((cap, hidden), BF16),
            pltpu.VMEM((experts, feats), BF16),
            pltpu.VMEM((experts, cap), I32),
            pltpu.VMEM((2, experts, SLOTS, LANES), BF16),
            pltpu.VMEM((2, experts, SLOTS, LANES), BF16),
            pltpu.VMEM((experts, SLOTS, LANES), BF16),
            pltpu.VMEM((4, 2 * SLOTS, LANES), BF16),
            pltpu.VMEM((4, 2 * SLOTS, LANES), BF16),
            pltpu.VMEM((cap, LANES), BF16),
            pltpu.VMEM((cap, LANES), BF16),
            pltpu.VMEM((cap, LANES), BF16),
            pltpu.VMEM((cap, LANES), BF16),
            pltpu.VMEM((cap, LANES), BF16),
            pltpu.VMEM((cap, cap), BF16),
            pltpu.VMEM((cap, cap), BF16),
            pltpu.VMEM((blocks, cap, LANES), BF16),
            pltpu.VMEM((blocks, hidden, LANES), BF16),
            pltpu.VMEM((blocks, hidden, LANES), BF16),
            pltpu.VMEM((cap, hidden), F32),
            pltpu.VMEM((cap, hidden), F32),
            pltpu.VMEM((cap, hidden), F32),
            pltpu.VMEM((4 * SIDE, cap // LANES, LANES), F32),
            pltpu.VMEM((SIDE, cap // LANES, LANES), F32),
            pltpu.VMEM((experts, 1, LANES), F32),
            pltpu.VMEM((experts, 1, LANES), F32),
            pltpu.VMEM((experts, LANES), BF16),
            pltpu.VMEM((experts, experts, LANES), BF16),
            pltpu.VMEM((experts, LANES), F32),
            pltpu.VMEM((4, experts, LANES), F32),
            dma((6,)), dma(()), dma(()), dma(()), dma(()), dma(()),
            dma((2,)), dma((2,)), dma(()), dma((2,)), dma((experts,)), dma(()), dma(()),
            dma(()), dma(()), dma(()), dma(()), dma(()), dma(()), dma(()), dma(()),
            dma(()), dma((2, SIDE)), dma((2, SIDE, SIDE)), dma(()), dma(()),
            dma(()), dma(()), dma(()), dma(()),
            dma(()), dma(()), dma(()), dma(()), dma(()), dma(()),
        ],
        compiler_params=pltpu.CompilerParams(
            collective_id=0, has_side_effects=True, vmem_limit_bytes=48 * 2**20
        ),
        cost_estimate=pl.CostEstimate(
            flops=2 * cap * hidden * feats * blocks, bytes_accessed=4 * 2**20, transcendentals=0
        ),
        name="gated_moe_backward",
    )(
        *(
            pltpu.with_memory_space_constraint(v, pltpu.HBM)
            for v in (
                cotangent, activations, router_logits.T, saved_hidden, down_weight, router_weight.T, choices
            )
        )
    )
    return hidden_grad, token_grad, router_grad.T


def solution(mesh):
    placed = (
        P("expert", "tensor"),
        P("expert", "tensor"),
        P("expert", None),
        P(None, ("expert", "tensor")),
        P(("expert", "tensor"), None),
        P("tensor", None),
        P(),
    )
    return jax.shard_map(
        on_device,
        mesh=mesh,
        in_specs=placed,
        out_specs=(P(None, ("expert", "tensor")), P("expert", "tensor"), P("tensor", None)),
        check_vma=False,
    )
```

time: 110 us -> 96.4 us (0.88)
  local copies, waits for them, and re-layouts: 8.4 us -> 1.92 us
  Pallas kernels: 100 us -> 93.6 us
    pallas_call x1, Pallas kernels: 100 us -> 93.6 us  [on_device(): pl.pallas_call(kernel, out_shape=(jax.ShapeDtypeStruct((cap, hidden), BF1...]
    unnamed x14 -> x3, local copies, waits for them, and re-layouts: 7.72 us -> 1.92 us
where the time goes in v2:
time: 96.4 us; the launch traced here: 96.1 us
  Pallas kernels  93.6 us (97%)
  local copies, waits for them, and re-layouts  1.92 us (2%)
    pallas_call x1, Pallas kernels, on_device(): pl.pallas_call(kernel, out_shape=(jax.ShapeDtypeStruct((cap, hidden), BF1...  93.6 us

profile of v2, /device:TPU:1, one launch (start us, length us, event | category | flops | bytes accessed | tf_op | source)
XLA Modules:
  0.0 96.1 jit_solution(2176349322927307469)
XLA Ops:
  0.6 93.6 %gated_moe_backward.1 = (bf16[512,256]{1,0:T(8,128)(2,1)S(1)}, bf16[64,256]{1,0:T(8,128)(2,1)S(1)}, f32[16,256]{1,0:T(8,128)S(1)}) custom-call(bf16[64,256]{1,0:T(8,128)(2,1)} %cot_hbm.1, bf16[64,256]{1,0:T(8,128)(2,1)} %act_hbm.1, f32[16,64]{1,0:T(8,128)} %bitcast.4, bf16[512,256]{1,0:T(8,128)(2,1)} %saved_hbm.1, bf16[256,4096]{1,0:T(8,128)(2,1)} %w_hbm.1, ...), custom_call_target="tpu_custom_call" | custom-call | flops 1073741824 | bytes 4194304 | tf_op jit(solution)/shard_map/gated_moe_backward/pallas_call | solution.py:536
  94.2 0.7 copy.13
  94.9 0.6 copy.14
  95.5 0.6 copy.15

commit v3 on v2

--- a/solution.py
+++ b/solution.py
@@ -44,14 +44,14 @@
 def kernel(
     cot_hbm, act_hbm, logit_hbm, saved_hbm, w_hbm, rw_hbm, choice_hbm,
     hid_ref, tok_ref, rg_ref,
-    cot_ref, act_ref, logit_ref, saved_ref, saved_other, rw_ref, choice_ref,
+    cot_ref, act_ref, logit_ref, saved, rw_ref, choice_ref,
     cot_out, act_out, p_out, up, down, cot_own, cot_pair, act_own, p_own, p_pair,
-    hot_own, hot_pair, xbuf, w_self, w_other, acc_self, acc_other, part_in,
+    hot_own, hot_pair, xbuf, weights, acc, acc_out, part_core, part_chip,
     gate_one, gate_two, s_out, s_in, r_out, r_in, f_out, f_in,
     in_sem, w_sem, w_send, w_recv, saved_send, saved_recv,
     up_send, up_recv, near_send, hop_send, cot_recv, pair_send, pair_recv,
     act_send, act_recv, p_send, p_recv, p_two_send, p_two_recv, p_pair_send, p_pair_recv,
-    x_send, x_one, x_two, core_send, core_recv, one_send, one_recv, two_send, two_recv,
+    x_send, x_one, x_two, core_send, core_recv, chip_send, chip_recv, one_send, one_recv, two_send, two_recv,
     s_send, s_recv, r_send, r_recv, f_send, f_recv,
 ):
     me, xy = lax.axis_index("expert"), lax.axis_index("tensor")
@@ -63,6 +63,9 @@
     e = z // 2
     x, y = xy // SIDE, xy % SIDE
     other_core = z * 2 + (1 - h)
+    beside = x + 1 - 2 * (x % 2)
+    beside_xy = beside * SIDE + y
+    mirror_xy = (SIDE - 1 - x) * SIDE + y
     pair_z = z + 1 - 2 * (z % 2)
     pair = pair_z * 2 + h
     quarter = (z % 2) * 2 + h
@@ -95,7 +98,7 @@
 
     arrays = {
         "choice": (choice_hbm, choice_ref), "cot": (cot_hbm, cot_ref), "act": (act_hbm, act_ref),
-        "logit": (logit_hbm, logit_ref), "saved": (saved_hbm, saved_ref), "rw": (rw_hbm, rw_ref),
+        "logit": (logit_hbm, logit_ref), "saved": (saved_hbm, saved.at[0]), "rw": (rw_hbm, rw_ref),
     }
 
     def load(*names):
@@ -150,15 +153,23 @@
     pl.semaphore_wait(barrier, greeted)
 
     slots_of_core = pl.ds(pl.multiple_of(h * SLOTS, SLOTS), SLOTS)
-    for c in range(2):
+
+    def relay_up(c, j):
         remote(
-            cot_out.at[c, pl.ds(far + 1, far - c)], up.at[pl.ds(0, far - c), slots_of_core], up_send.at[0],
-            up_recv.at[0], at_z(far) * 2 + c,
+            cot_out.at[c, far + 1 + j], up.at[j, slots_of_core], up_send, up_recv.at[0, j], at_z(far) * 2 + c
         ).start()
+
+    def relay_down(c, j):
         remote(
-            cot_out.at[c, pl.ds(2 * far + 1 - c, far - 1 + c)], down.at[pl.ds(1 - c, far - 1 + c), slots_of_core],
-            up_send.at[1], up_recv.at[1], at_z(-far) * 2 + c,
+            cot_out.at[c, 2 * far + j], down.at[j, slots_of_core], up_send, up_recv.at[1, j], at_z(-far) * 2 + c
         ).start()
+
+    relay_up(0, far - 1)
+    relay_down(1, 0)
+    for j in range(1, far):
+        for c in range(2):
+            relay_up(c, far - 1 - j)
+            relay_down(c, j)
     pair_rows = 2 * SLOTS
 
     def rows_from(k):
@@ -172,18 +183,31 @@
             ).start()
     remote(cot_out.at[1 - h, 0], cot_own.at[mine], near_send, cot_recv.at[0], other_core).start()
     pltpu.make_async_copy(cot_out.at[h, 0], cot_own.at[mine], cot_recv.at[0]).start()
-    load("act", "logit")
     later("near", cot_own.at[pl.ds(0, (2 * len(near_steps) + 1) * SLOTS)], near_send)
 
-    blocks = w_self.shape[0]
-    for b in range(blocks):
-        pltpu.make_async_copy(
-            w_hbm.at[:, pl.ds(pl.multiple_of(b * 2 * LANES + h * LANES, LANES), LANES)],
-            w_self.at[b], w_sem,
-        ).start()
-    later("w", w_self, w_sem)
-
-    load("saved", "rw")
+    def half_of(px, c, j):
+        return w_hbm.at[:, pl.ds(pl.multiple_of((px * SIDE + j) * 2 * LANES + c * LANES, LANES), LANES)]
+
+    load("act", "logit", "saved", "rw")
+    for p, px in enumerate((x, SIDE - 1 - x)):
+        for j in range(SIDE):
+            pltpu.make_async_copy(half_of(px, h, j), weights.at[0, p * SIDE + j], w_sem).start()
+    for p, px in enumerate((beside, SIDE - 1 - beside)):
+        for j in range(SIDE):
+            at = p * SIDE + j
+            remote(half_of(px, h, j), weights.at[2, at], w_send, w_recv.at[1], me, beside_xy).start()
+            remote(half_of(px, 1 - h, j), weights.at[3, at], w_send, w_recv.at[2], other_core, beside_xy).start()
+    for p, px in enumerate((x, SIDE - 1 - x)):
+        for j in range(SIDE):
+            remote(half_of(px, 1 - h, j), weights.at[1, p * SIDE + j], w_send, w_recv.at[0], other_core).start()
+    remote(saved_hbm, saved.at[2], saved_send, saved_recv.at[1], me, beside_xy).start()
+    remote(saved_hbm, saved.at[1], saved_send, saved_recv.at[0], other_core).start()
+    later("w0", weights.at[0], w_sem)
+    later("w_send", weights.at[pl.ds(0, 3)], w_send)
+    later("saved_send", saved.at[pl.ds(0, 3)], saved_send)
+    for n in range(3):
+        later(f"w{n + 1}", weights.at[n + 1], w_recv.at[n])
+        later(f"saved{n + 1}", saved.at[n + 1], saved_recv.at[n])
 
     finish("act")
     act_slots = dot(pick_bf, act_ref[...], TN).astype(BF16)
@@ -218,18 +242,6 @@
             remote(p_out.at[k], p_own.at[mine], p_send, p_recv, at_z(k) * 2 + c).start()
 
     def send_rest():
-        for m in range(SIDE - 1, 0, -1):
-            p_to(m * SIDE + y)
-
-        @pl.when(y != 0)
-        def _():
-            p_to(y)
-
-        @pl.when(y == 0)
-        def _():
-            remote(p_out.at[0], p_own.at[mine], p_send, p_recv, other_core).start()
-            pltpu.make_async_copy(p_out.at[0], p_own.at[mine], p_recv).start()
-
         act_to(middle)
         lax.fori_loop(1, middle, act_each, 0)
         remote(act_out.at[1 - h, 0], act_own.at[mine], act_send, act_recv, other_core).start()
@@ -237,6 +249,19 @@
         later("act_send", act_own.at[pl.ds(0, cap - SLOTS)], act_send)
         later("act_slots", act_own, act_recv)
         waits["p_send"] = p_sent
+
+    def send_p():
+        for m in range(SIDE - 1, 0, -1):
+            p_to(m * SIDE + y)
+
+        @pl.when(y != 0)
+        def _():
+            p_to(y)
+
+        @pl.when(y == 0)
+        def _():
+            remote(p_out.at[0], p_own.at[mine], p_send, p_recv, other_core).start()
+            pltpu.make_async_copy(p_out.at[0], p_own.at[mine], p_recv).start()
 
     def p_sent():
         sends = 2 * experts // SIDE
@@ -268,58 +293,34 @@
     later("pair", cot_pair, pair_recv)
 
     def hop_up(j):
+        wait_bytes(up.at[j], up_recv.at[0, j])
         remote(
-            up.at[j], cot_own.at[rows_from(far)], hop_send.at[0], cot_recv.at[far + 1 + j], at_z(1 + j) * 2 + h
+            up.at[j], cot_own.at[rows_from(far)], hop_send, cot_recv.at[far + 1 + j], at_z(1 + j) * 2 + h
         ).start()
 
     def hop_down(j):
+        wait_bytes(down.at[j], up_recv.at[1, j])
         remote(
-            down.at[j], cot_own.at[rows_from(-far)], hop_send.at[1], cot_recv.at[2 * far + j], at_z(j - far) * 2 + h
+            down.at[j], cot_own.at[rows_from(-far)], hop_send, cot_recv.at[2 * far + j], at_z(j - far) * 2 + h
         ).start()
 
     for k in (0, 1, -1, 2, -2):
         share(k)
-    most, fewer = pl.ds(0, far), pl.ds(0, far - 1)
-
     @pl.when(h == 0)
     def _():
-        wait_bytes(up.at[most], up_recv.at[0])
         hop_up(far - 1)
 
     @pl.when(h == 1)
     def _():
-        wait_bytes(up.at[fewer], up_recv.at[0])
-
-    for j in range(far - 2, -1, -1):
-        hop_up(j)
-
-    @pl.when(h == 1)
-    def _():
-        wait_bytes(down.at[most], up_recv.at[1])
         hop_down(0)
 
-    @pl.when(h == 0)
-    def _():
-        wait_bytes(down.at[fewer], up_recv.at[1])
-
     for j in range(1, far):
+        hop_up(far - 1 - j)
         hop_down(j)
-
-    def hopped():
-        @pl.when(h == 0)
-        def _():
-            wait_bytes(up.at[most], hop_send.at[0])
-            wait_bytes(down.at[fewer], hop_send.at[1])
-
-        @pl.when(h == 1)
-        def _():
-            wait_bytes(up.at[fewer], hop_send.at[0])
-            wait_bytes(down.at[most], hop_send.at[1])
-
-    waits["hop"] = hopped
-    relayed = cot_own.at[pl.ds(0, (2 * far - 1) * SLOTS)]
-    later("up_send", relayed, up_send.at[0])
-    later("down_send", relayed, up_send.at[1])
+    relayed = cot_own.at[pl.ds(0, 2 * (2 * far - 1) * SLOTS)]
+    send_p()
+    later("up_send", relayed, up_send)
+    later("hop_send", relayed, hop_send)
 
     wanted = choice_ref[pl.ds(e, 1), :].astype(F32)
     wanted_col = jnp.transpose(jnp.broadcast_to(wanted, (LANES, cap)))[:, :1].astype(I32)
@@ -336,81 +337,71 @@
 
     for k in (3, -3, 4, -4, 5, -5, 6, -6, 7, -7, 8):
         share(k)
+    half = cap // 2
     picked = dot(hot_own[...], cot_own[...])
     finish("pair")
-    xbuf[xy] = (picked + dot(hot_pair[...], cot_pair[...])).astype(BF16)
-
-    half = cap // 2
+
     order = (1, 3, 2)
 
     def rows_of(first):
         return pl.ds(first * half, half)
 
-    def along(first, i, j):
-        return at_xy(i, j) if first == 0 else at_xy(j, i)
-
-    def send_block(first, block, recv, i, j):
-        ref = xbuf.at[block, rows_of(first)]
-        remote(ref, ref, x_send, recv, me, along(first, i, j)).start()
-
-    for i in order:
-        for first in range(2):
-            send_block(first, xy, x_one.at[first, i], i, 0)
+    def send_block(first, src, dst, recv, to):
+        remote(xbuf.at[src, rows_of(first)], xbuf.at[dst, rows_of(first)], x_send, recv, me, to).start()
+
+    def from_y(j):
+        return (y - j + SIDE) % SIDE
+
+    for first in range(2):
+        rows = slice(first * half, (first + 1) * half)
+        xbuf[y, rows_of(first), :] = (picked[rows] + dot(hot_pair[rows, :], cot_pair[...])).astype(BF16)
+        if first == 0:
+            send_block(0, y, SIDE + y, x_one.at[0, 0], mirror_xy)
+        else:
+            for j in order:
+                send_block(1, y, y, x_one.at[1, j], at_xy(0, j))
     for j in order:
-        for first in range(2):
-            send_block(first, xy, x_two.at[first, 0, j], 0, j)
-    for b in range(blocks):
-        remote(
-            w_hbm.at[:, pl.ds(pl.multiple_of(b * 2 * LANES + (1 - h) * LANES, LANES), LANES)],
-            w_other.at[b], w_send, w_recv, other_core,
-        ).start()
-    later("w_send", w_other, w_send)
-    later("w_other", w_other, w_recv)
-    remote(saved_hbm, saved_other, saved_send, saved_recv, other_core).start()
-    later("saved_send", saved_other, saved_send)
-    later("saved_other", saved_other, saved_recv)
-
-    later("x_send", xbuf.at[pl.ds(0, SIDE * SIDE - 1)], x_send)
-
-    def relay(i):
-        for first in range(2):
-            block = along(first, -i, 0)
-            wait_bytes(xbuf.at[block, rows_of(first)], x_one.at[first, i])
-            for j in order:
-                send_block(first, block, x_two.at[first, i, j], 0, j)
-
+        send_block(0, y, y, x_two.at[0, 0, j], at_xy(0, j))
+    send_block(1, y, SIDE + y, x_two.at[1, 0, 0], mirror_xy)
+    later("x_send", xbuf.at[pl.ds(0, 2 * SIDE - 1)], x_send)
     send_rest()
-    relay(1)
-    relay(3)
-    relay(2)
+    wait_bytes(xbuf.at[SIDE + y, rows_of(0)], x_one.at[0, 0])
+    for j in order:
+        send_block(0, SIDE + y, SIDE + y, x_two.at[0, 1, j], at_xy(0, j))
+    for j in order:
+        wait_bytes(xbuf.at[from_y(j), rows_of(1)], x_one.at[1, j])
+        send_block(1, from_y(j), SIDE + from_y(j), x_two.at[1, 0, j], mirror_xy)
     share_p()
-
-    finish("w")
-    finish("w_other")
-
-    def product(first, blocks_at, weights):
+    finish("saved2")
+    remote(saved.at[2], saved.at[3], saved_send, saved_recv.at[2], other_core).start()
+    for n in range(4):
+        finish(f"w{n}")
+
+    def product(p, first, n):
+        blocks_at = range(p * SIDE, (p + 1) * SIDE)
         lhs = jnp.concatenate([xbuf[b, first * half : (first + 1) * half, :] for b in blocks_at], axis=1)
-        rhs = jnp.concatenate([weights[b] for b in blocks_at], axis=1)
+        rhs = jnp.concatenate([weights[n, b] for b in blocks_at], axis=1)
         return dot(lhs, rhs, NT)
 
     def span(first):
         return slice(first * half, (first + 1) * half)
 
+    for j in order:
+        wait_bytes(xbuf.at[from_y(j), rows_of(0)], x_two.at[0, 0, j])
     for first in range(2):
-        at = [along(first, -i, 0) for i in range(SIDE)]
-        acc_other[span(first), :] = product(first, at, w_other)
-        acc_self[span(first), :] = product(first, at, w_self)
-    for j in order:
-        for first in range(2):
-            at = [along(first, -i, -j) for i in range(SIDE)]
-            for i in range(SIDE):
-                wait_bytes(xbuf.at[at[i], rows_of(first)], x_two.at[first, i, j])
-            acc_other[span(first), :] += product(first, at, w_other)
-            acc_self[span(first), :] += product(first, at, w_self)
+        for n in range(4):
+            acc[n, span(first), :] = product(0, first, n)
+    for first in range(2):
+        for j in order if first == 0 else (0, *order):
+            sem = x_two.at[0, 1, j] if first == 0 else x_two.at[1, 0, j]
+            wait_bytes(xbuf.at[SIDE + from_y(j), rows_of(first)], sem)
+        for n in range(4):
+            acc[n, span(first), :] += product(1, first, n)
 
     finish("saved")
-    finish("saved_other")
-    prod = saved_ref[...].astype(F32) * acc_self[...] + saved_other[...].astype(F32) * acc_other[...]
+    finish("saved1")
+    finish("saved3")
+    prod = sum(saved[n].astype(F32) * acc[n] for n in range(4))
     gate = jnp.sum(jnp.transpose(prod[:, :LANES] + prod[:, LANES:]), axis=0, keepdims=True)
     pieces = cap // LANES
     slot_one = x * 4 + quarter
@@ -426,12 +417,14 @@
         remote(gate_two.at[y], gate_two.at[y], two_send, two_recv, me, at_xy(0, j)).start()
     later("two_send", gate_two.at[pl.ds(0, SIDE - 1)], two_send)
 
-    for first in range(2):
-        remote(
-            acc_other.at[rows_of(first)], part_in.at[rows_of(first)], core_send, core_recv, other_core
-        ).start()
-    later("core_send", acc_other, core_send)
-    later("part", part_in, core_recv)
+    remote(acc.at[1], part_core, core_send, core_recv, other_core).start()
+    for n, to in enumerate((me, other_core)):
+        acc_out[n] = acc[2 + n].astype(BF16)
+        remote(acc_out.at[n], part_chip.at[n], chip_send.at[n], chip_recv.at[n], to, beside_xy).start()
+        later(f"chip_send{n}", part_chip.at[n], chip_send.at[n])
+        later(f"part{n}", part_chip.at[n], chip_recv.at[n])
+    later("core_send", part_core, core_send)
+    later("part", part_core, core_recv)
 
     finish("p_slots")
     p_to_pair = remote(p_own, p_pair, p_pair_send, p_pair_recv, pair)
@@ -443,14 +436,14 @@
     mine_row = iota((experts, cap), 0) == e
     p_mine = jnp.sum(jnp.where(mine_row, p_slot, 0.0), axis=0, keepdims=True)
     slope = p_mine * (jnp.where(mine_row, 1.0, 0.0) - p_slot)
+    slope_row = dot(jnp.concatenate(thirds(slope), axis=0).astype(BF16), hot_own[...], NT)
+    slope_row = slope_row[:experts] + slope_row[experts : 2 * experts] + slope_row[2 * experts :]
     finish("act_slots")
+    act_row = dot(hot_own[...], act_own[...]).astype(BF16)
 
     wait_bytes(gate_two.at[pl.ds(0, SIDE - 1)], two_recv)
     total = jnp.sum(gate_two[...], axis=0)
     total_row = jnp.concatenate([total[k : k + 1, :] for k in range(pieces)], axis=1)
-    rows3 = jnp.concatenate([total_row, jnp.zeros((7, cap), F32)], axis=0)
-    s_three = dot(jnp.concatenate(thirds(rows3), axis=0).astype(BF16), hot_own[...])
-    s_slot = s_three[0:1] + s_three[8:9] + s_three[16:17]
 
     def back(name, out, into, send, recv):
         def one(k):
@@ -469,11 +462,14 @@
         later(name + "_send", into.at[pl.ds(0, experts - 1)], send)
         later(name, into.at[pl.ds(0, experts - 1)], recv)
 
-    w_slot = s_slot * slope
-    r_three = dot(jnp.concatenate(thirds(w_slot), axis=0).astype(BF16), act_own[...])
+    w_row = total_row * slope_row
+    r_three = dot(jnp.concatenate(thirds(w_row), axis=0).astype(BF16), act_row)
     r_part = r_three[:experts] + r_three[experts : 2 * experts] + r_three[2 * experts :]
     r_out[...] = r_part.astype(BF16)
     back("r", lambda k: r_out, r_in, r_send, r_recv)
+    rows3 = jnp.concatenate([total_row, jnp.zeros((7, cap), F32)], axis=0)
+    s_three = dot(jnp.concatenate(thirds(rows3), axis=0).astype(BF16), hot_own[...])
+    s_slot = s_three[0:1] + s_three[8:9] + s_three[16:17]
     slot_at = iota((experts, cap), 1)
     of_owner = (jnp.right_shift(slot_at, slot_shift + 1) == iota((experts, cap), 0)) & (
         (jnp.right_shift(slot_at, slot_shift) & 1) == h
@@ -493,7 +489,10 @@
     gates = dot(hot_own[...], p_own[...]) + dot(hot_pair[...], p_pair[...])
     gate_col = jnp.sum(jnp.where(iota((cap, LANES), 1) == e, gates, 0.0), axis=1, keepdims=True)
     finish("part")
-    hid_ref[...] = (gate_col * (acc_self[...] + part_in[...])).astype(BF16)
+    finish("part0")
+    finish("part1")
+    pre = acc[0] + part_core[...] + (part_chip[0].astype(F32) + part_chip[1].astype(F32))
+    hid_ref[...] = (gate_col * pre).astype(BF16)
 
     finish("rw")
     finish("s")
@@ -522,6 +521,17 @@
         finish(name)
 
 
+def write(hid_ref, tok_ref, rg_ref, hid_out, tok_out, rg_out, sem):
+    copies = [
+        pltpu.make_async_copy(src, dst, sem.at[n])
+        for n, (src, dst) in enumerate(((hid_ref, hid_out), (tok_ref, tok_out), (rg_ref, rg_out)))
+    ]
+    for copy in copies:
+        copy.start()
+    for copy in copies:
+        copy.wait()
+
+
 def on_device(
     cotangent, activations, router_logits, saved_hidden, down_weight, router_weight, choices
 ):
@@ -533,21 +543,21 @@
     vmem = pl.BlockSpec(memory_space=pltpu.VMEM)
     hbm = pl.BlockSpec(memory_space=pltpu.HBM)
     dma = pltpu.SemaphoreType.DMA
-    hidden_grad, token_grad, router_grad = pl.pallas_call(
+    shapes = (
+        jax.ShapeDtypeStruct((cap, hidden), BF16),
+        jax.ShapeDtypeStruct((own_tokens, feats), BF16),
+        jax.ShapeDtypeStruct((experts, feats), F32),
+    )
+    grads = pl.pallas_call(
         kernel,
-        out_shape=(
-            jax.ShapeDtypeStruct((cap, hidden), BF16),
-            jax.ShapeDtypeStruct((own_tokens, feats), BF16),
-            jax.ShapeDtypeStruct((experts, feats), F32),
-        ),
+        out_shape=shapes,
         in_specs=[hbm] * 7,
         out_specs=(vmem, vmem, vmem),
         scratch_shapes=[
             pltpu.VMEM((own_tokens, feats), BF16),
             pltpu.VMEM((own_tokens, feats), BF16),
             pltpu.VMEM((experts, own_tokens), F32),
-            pltpu.VMEM((cap, hidden), BF16),
-            pltpu.VMEM((cap, hidden), BF16),
+            pltpu.VMEM((4, cap, hidden), BF16),
             pltpu.VMEM((experts, feats), BF16),
             pltpu.VMEM((experts, cap), I32),
             pltpu.VMEM((2, experts, SLOTS, LANES), BF16),
@@ -562,12 +572,12 @@
             pltpu.VMEM((cap, LANES), BF16),
             pltpu.VMEM((cap, cap), BF16),
             pltpu.VMEM((cap, cap), BF16),
-            pltpu.VMEM((blocks, cap, LANES), BF16),
-            pltpu.VMEM((blocks, hidden, LANES), BF16),
-            pltpu.VMEM((blocks, hidden, LANES), BF16),
+            pltpu.VMEM((2 * SIDE, cap, LANES), BF16),
+            pltpu.VMEM((4, 2 * SIDE, hidden, LANES), BF16),
+            pltpu.VMEM((4, cap, hidden), F32),
+            pltpu.VMEM((2, cap, hidden), BF16),
             pltpu.VMEM((cap, hidden), F32),
-            pltpu.VMEM((cap, hidden), F32),
-            pltpu.VMEM((cap, hidden), F32),
+            pltpu.VMEM((2, cap, hidden), BF16),
             pltpu.VMEM((4 * SIDE, cap // LANES, LANES), F32),
             pltpu.VMEM((SIDE, cap // LANES, LANES), F32),
             pltpu.VMEM((experts, 1, LANES), F32),
@@ -576,10 +586,10 @@
             pltpu.VMEM((experts, experts, LANES), BF16),
             pltpu.VMEM((experts, LANES), F32),
             pltpu.VMEM((4, experts, LANES), F32),
-            dma((6,)), dma(()), dma(()), dma(()), dma(()), dma(()),
-            dma((2,)), dma((2,)), dma(()), dma((2,)), dma((experts,)), dma(()), dma(()),
+            dma((6,)), dma(()), dma(()), dma((3,)), dma(()), dma((3,)),
+            dma(()), dma((2, 4)), dma(()), dma(()), dma((experts,)), dma(()), dma(()),
             dma(()), dma(()), dma(()), dma(()), dma(()), dma(()), dma(()), dma(()),
-            dma(()), dma((2, SIDE)), dma((2, SIDE, SIDE)), dma(()), dma(()),
+            dma(()), dma((2, SIDE)), dma((2, 2, SIDE)), dma(()), dma(()), dma((2,)), dma((2,)),
             dma(()), dma(()), dma(()), dma(()),
             dma(()), dma(()), dma(()), dma(()), dma(()), dma(()),
         ],
@@ -598,6 +608,15 @@
             )
         )
     )
+    hidden_grad, token_grad, router_grad = pl.pallas_call(
+        write,
+        out_shape=shapes,
+        in_specs=[vmem] * 3,
+        out_specs=(hbm, hbm, hbm),
+        scratch_shapes=[dma((3,))],
+        compiler_params=pltpu.CompilerParams(vmem_limit_bytes=2 * 2**20),
+        name="write_gradients",
+    )(*grads)
     return hidden_grad, token_grad, router_grad.T
 
 

time: 96.4 us -> 87.5 us (0.908)
  Pallas kernels: 93.6 us -> 86.6 us
  local copies, waits for them, and re-layouts: 1.92 us -> 0 us
    pallas_call x1 -> x2, Pallas kernels: 93.6 us -> 86.6 us  [the longest x1 85.9 us: on_device(): pl.pallas_call(kernel, out_shape=shapes, in_specs=[hbm] * 7, out_specs=(v...]
    unnamed x3 -> x0, local copies, waits for them, and re-layouts: 1.92 us -> none
where the time goes in v3:
time: 87.5 us; the launch traced here: 87.3 us
  Pallas kernels  86.6 us (99%)
    pallas_call x1, Pallas kernels, on_device(): pl.pallas_call(kernel, out_shape=shapes, in_specs=[hbm] * 7, out_specs=(v...  85.9 us

profile of v3, /device:TPU:1, one launch (start us, length us, event | category | flops | bytes accessed | tf_op | source)
XLA Modules:
  0.0 87.3 jit_solution(10934566375557545354)
XLA Ops:
  0.6 85.9 %gated_moe_backward.1 = (bf16[512,256]{1,0:T(8,128)(2,1)S(1)}, bf16[64,256]{1,0:T(8,128)(2,1)S(1)}, f32[16,256]{1,0:T(8,128)S(1)}) custom-call(bf16[64,256]{1,0:T(8,128)(2,1)} %cot_hbm.1, bf16[64,256]{1,0:T(8,128)(2,1)} %act_hbm.1, f32[16,64]{1,0:T(8,128)} %bitcast.4, bf16[512,256]{1,0:T(8,128)(2,1)} %saved_hbm.1, bf16[256,4096]{1,0:T(8,128)(2,1)} %w_hbm.1, ...), custom_call_target="tpu_custom_call" | custom-call | flops 1073741824 | bytes 4194304 | tf_op jit(solution)/shard_map/gated_moe_backward/pallas_call | solution.py:551
  86.5 0.7 write_gradients.1

commit v4 on v3

--- a/solution.py
+++ b/solution.py
@@ -47,12 +47,12 @@
     cot_ref, act_ref, logit_ref, saved, rw_ref, choice_ref,
     cot_out, act_out, p_out, up, down, cot_own, cot_pair, act_own, p_own, p_pair,
     hot_own, hot_pair, xbuf, weights, acc, acc_out, part_core, part_chip,
-    gate_one, gate_two, s_out, s_in, r_out, r_in, f_out, f_in,
+    gate_one, gate_two, s_out, s_in, r_out, r_mid, r_in, f_out, f_in,
     in_sem, w_sem, w_send, w_recv, saved_send, saved_recv,
     up_send, up_recv, near_send, hop_send, cot_recv, pair_send, pair_recv,
     act_send, act_recv, p_send, p_recv, p_two_send, p_two_recv, p_pair_send, p_pair_recv,
     x_send, x_one, x_two, core_send, core_recv, chip_send, chip_recv, one_send, one_recv, two_send, two_recv,
-    s_send, s_recv, r_send, r_recv, f_send, f_recv,
+    s_send, s_recv, r_send, r_mid_send, r_recv, f_send, f_recv,
 ):
     me, xy = lax.axis_index("expert"), lax.axis_index("tensor")
     groups = lax.axis_size("expert")
@@ -391,22 +391,24 @@
     for first in range(2):
         for n in range(4):
             acc[n, span(first), :] = product(0, first, n)
+    finish("saved")
+    finish("saved1")
+    finish("saved3")
+    slot_one = x * 4 + quarter
+    pieces = half // LANES
     for first in range(2):
         for j in order if first == 0 else (0, *order):
             sem = x_two.at[0, 1, j] if first == 0 else x_two.at[1, 0, j]
             wait_bytes(xbuf.at[SIDE + from_y(j), rows_of(first)], sem)
+        prod = 0.0
         for n in range(4):
-            acc[n, span(first), :] += product(1, first, n)
-
-    finish("saved")
-    finish("saved1")
-    finish("saved3")
-    prod = sum(saved[n].astype(F32) * acc[n] for n in range(4))
-    gate = jnp.sum(jnp.transpose(prod[:, :LANES] + prod[:, LANES:]), axis=0, keepdims=True)
-    pieces = cap // LANES
-    slot_one = x * 4 + quarter
-    for k in range(pieces):
-        gate_one[slot_one, k : k + 1, :] = gate[0:1, k * LANES : (k + 1) * LANES]
+            pre = acc[n, span(first), :] + product(1, first, n)
+            acc[n, span(first), :] = pre
+            prod += saved[n, span(first), :].astype(F32) * pre
+        gate = jnp.sum(jnp.transpose(prod[:, :LANES] + prod[:, LANES:]), axis=0, keepdims=True)
+        for k in range(pieces):
+            gate_one[slot_one, first * pieces + k : first * pieces + k + 1, :] = gate[:, k * LANES : (k + 1) * LANES]
+
     for i in (2, 1, 3, 0):
         for q in quarters + (() if i == 0 else (me,)):
             remote(gate_one.at[slot_one], gate_one.at[slot_one], one_send, one_recv, q, at_xy(i, 0)).start()
@@ -443,30 +445,15 @@
 
     wait_bytes(gate_two.at[pl.ds(0, SIDE - 1)], two_recv)
     total = jnp.sum(gate_two[...], axis=0)
-    total_row = jnp.concatenate([total[k : k + 1, :] for k in range(pieces)], axis=1)
-
-    def back(name, out, into, send, recv):
-        def one(k):
-            to = (z + 2 * k) % chips
-            remote(out(to // 2), into.at[e], send, recv, to * 2 + h).start()
-
-        middle = experts // 2
-        one(middle)
-
-        def each(j, carry):
-            one(middle - j)
-            one(middle + j)
-            return carry
-
-        lax.fori_loop(1, middle, each, 0)
-        later(name + "_send", into.at[pl.ds(0, experts - 1)], send)
-        later(name, into.at[pl.ds(0, experts - 1)], recv)
+    total_row = jnp.concatenate([total[k : k + 1, :] for k in range(2 * pieces)], axis=1)
 
     w_row = total_row * slope_row
     r_three = dot(jnp.concatenate(thirds(w_row), axis=0).astype(BF16), act_row)
     r_part = r_three[:experts] + r_three[experts : 2 * experts] + r_three[2 * experts :]
     r_out[...] = r_part.astype(BF16)
-    back("r", lambda k: r_out, r_in, r_send, r_recv)
+    for n, k in enumerate((middle, 2, -2, 1, -1)):
+        remote(r_out, r_in.at[n], r_send, r_recv.at[min(n, 1)], at_z(k) * 2 + h).start()
+    later("r_send", r_in.at[pl.ds(0, 5)], r_send)
     rows3 = jnp.concatenate([total_row, jnp.zeros((7, cap), F32)], axis=0)
     s_three = dot(jnp.concatenate(thirds(rows3), axis=0).astype(BF16), hot_own[...])
     s_slot = s_three[0:1] + s_three[8:9] + s_three[16:17]
@@ -481,9 +468,17 @@
     for k in range(experts):
         s_out[k] = s_rows[k : k + 1, :]
 
-    back("s", lambda k: s_out.at[k], s_in, s_send, s_recv)
-    r_in[e] = r_out[...]
+    for k in [middle] + [j * sign for j in range(middle - 1, 0, -1) for sign in (1, -1)]:
+        remote(s_out.at[at_z(k) // 2], s_in.at[e], s_send, s_recv, at_z(k) * 2 + h).start()
+    later("s_send", s_in.at[pl.ds(0, experts - 1)], s_send)
+    later("s", s_in.at[pl.ds(0, experts - 1)], s_recv)
     s_in[e] = s_out[e]
+    wait_bytes(r_in.at[pl.ds(1, 4)], r_recv.at[1])
+    f_out[...] = r_part + sum(r_in[n].astype(F32) for n in range(1, 5))
+    r_mid[...] = f_out[...].astype(BF16)
+    for n, k in enumerate((5, -5)):
+        remote(r_mid, r_in.at[5 + n], r_mid_send, r_recv.at[2], at_z(k) * 2 + h).start()
+    later("r_mid_send", r_in.at[pl.ds(5, 2)], r_mid_send)
 
     finish("p_pair")
     gates = dot(hot_own[...], p_own[...]) + dot(hot_pair[...], p_pair[...])
@@ -493,6 +488,14 @@
     finish("part1")
     pre = acc[0] + part_core[...] + (part_chip[0].astype(F32) + part_chip[1].astype(F32))
     hid_ref[...] = (gate_col * pre).astype(BF16)
+
+    wait_bytes(r_in.at[0], r_recv.at[0])
+    wait_bytes(r_in.at[pl.ds(5, 2)], r_recv.at[2])
+    f_out[...] += r_in[0].astype(F32) + (r_in[5].astype(F32) + r_in[6].astype(F32))
+    f_in[quarter] = f_out[...]
+    for q in quarters:
+        remote(f_out, f_in.at[quarter], f_send, f_recv, q).start()
+    later("f_send", f_in.at[pl.ds(0, len(quarters))], f_send)
 
     finish("rw")
     finish("s")
@@ -507,12 +510,6 @@
     logit_grad = (probs * (score - inner)).astype(BF16)
     tok_ref[...] = dot(logit_grad, rw_ref[...], TN).astype(BF16)
 
-    finish("r")
-    f_out[...] = jnp.sum(r_in[...].astype(F32), axis=0)
-    f_in[quarter] = f_out[...]
-    for q in quarters:
-        remote(f_out, f_in.at[quarter], f_send, f_recv, q).start()
-    later("f_send", f_in.at[pl.ds(0, len(quarters))], f_send)
     wait_bytes(f_in.at[pl.ds(0, len(quarters))], f_recv)
     rg_ref[:, :LANES] = f_in[0] + f_in[2]
     rg_ref[:, LANES:] = f_in[1] + f_in[3]
@@ -583,7 +580,8 @@
             pltpu.VMEM((experts, 1, LANES), F32),
             pltpu.VMEM((experts, 1, LANES), F32),
             pltpu.VMEM((experts, LANES), BF16),
-            pltpu.VMEM((experts, experts, LANES), BF16),
+            pltpu.VMEM((experts, LANES), BF16),
+            pltpu.VMEM((7, experts, LANES), BF16),
             pltpu.VMEM((experts, LANES), F32),
             pltpu.VMEM((4, experts, LANES), F32),
             dma((6,)), dma(()), dma(()), dma((3,)), dma(()), dma((3,)),
@@ -591,7 +589,7 @@
             dma(()), dma(()), dma(()), dma(()), dma(()), dma(()), dma(()), dma(()),
             dma(()), dma((2, SIDE)), dma((2, 2, SIDE)), dma(()), dma(()), dma((2,)), dma((2,)),
             dma(()), dma(()), dma(()), dma(()),
-            dma(()), dma(()), dma(()), dma(()), dma(()), dma(()),
+            dma(()), dma(()), dma(()), dma(()), dma((3,)), dma(()), dma(()),
         ],
         compiler_params=pltpu.CompilerParams(
             collective_id=0, has_side_effects=True, vmem_limit_bytes=48 * 2**20

time: 87.5 us -> 87.1 us (level)
  no operation moved by 1% of the time
where the time goes in v4:
time: 87.1 us; the launch traced here: 86.9 us
  Pallas kernels  86.2 us (99%)
    pallas_call x1, Pallas kernels, on_device(): pl.pallas_call(kernel, out_shape=shapes, in_specs=[hbm] * 7, out_specs=(v...  85.5 us

profile of v4, /device:TPU:1, one launch (start us, length us, event | category | flops | bytes accessed | tf_op | source)
XLA Modules:
  0.0 86.9 jit_solution(6013536240354500647)
XLA Ops:
  0.6 85.5 %gated_moe_backward.1 = (bf16[512,256]{1,0:T(8,128)(2,1)S(1)}, bf16[64,256]{1,0:T(8,128)(2,1)S(1)}, f32[16,256]{1,0:T(8,128)S(1)}) custom-call(bf16[64,256]{1,0:T(8,128)(2,1)} %cot_hbm.1, bf16[64,256]{1,0:T(8,128)(2,1)} %act_hbm.1, f32[16,64]{1,0:T(8,128)} %bitcast.4, bf16[512,256]{1,0:T(8,128)(2,1)} %saved_hbm.1, bf16[256,4096]{1,0:T(8,128)(2,1)} %w_hbm.1, ...), custom_call_target="tpu_custom_call" | custom-call | flops 1073741824 | bytes 4194304 | tf_op jit(solution)/shard_map/gated_moe_backward/pallas_call | solution.py:548
  86.1 0.7 write_gradients.1

commit v5 on v4

--- a/solution.py
+++ b/solution.py
@@ -164,23 +164,23 @@
             cot_out.at[c, 2 * far + j], down.at[j, slots_of_core], up_send, up_recv.at[1, j], at_z(-far) * 2 + c
         ).start()
 
+    pair_rows = 2 * SLOTS
+
+    def rows_from(k):
+        return pl.ds(pl.multiple_of(((e - k + experts) % experts) * pair_rows, pair_rows), pair_rows)
+
+    mine = pl.ds(pl.multiple_of(e * pair_rows + h * SLOTS, SLOTS), SLOTS)
+    for k in near_steps:
+        for c in range(2):
+            remote(
+                cot_out.at[c, k % experts], cot_own.at[mine], near_send, cot_recv.at[k % experts], at_z(k) * 2 + c
+            ).start()
     relay_up(0, far - 1)
     relay_down(1, 0)
     for j in range(1, far):
         for c in range(2):
             relay_up(c, far - 1 - j)
             relay_down(c, j)
-    pair_rows = 2 * SLOTS
-
-    def rows_from(k):
-        return pl.ds(pl.multiple_of(((e - k + experts) % experts) * pair_rows, pair_rows), pair_rows)
-
-    mine = pl.ds(pl.multiple_of(e * pair_rows + h * SLOTS, SLOTS), SLOTS)
-    for k in near_steps:
-        for c in range(2):
-            remote(
-                cot_out.at[c, k % experts], cot_own.at[mine], near_send, cot_recv.at[k % experts], at_z(k) * 2 + c
-            ).start()
     remote(cot_out.at[1 - h, 0], cot_own.at[mine], near_send, cot_recv.at[0], other_core).start()
     pltpu.make_async_copy(cot_out.at[h, 0], cot_own.at[mine], cot_recv.at[0]).start()
     later("near", cot_own.at[pl.ds(0, (2 * len(near_steps) + 1) * SLOTS)], near_send)

time: 87.1 us -> 87.4 us (level)
  no operation moved by 1% of the time
where the time goes in v5:
time: 87.4 us; the launch traced here: 87.1 us
  Pallas kernels  86.5 us (99%)
    pallas_call x1, Pallas kernels, on_device(): pl.pallas_call(kernel, out_shape=shapes, in_specs=[hbm] * 7, out_specs=(v...  85.8 us

profile of v5, /device:TPU:1, one launch (start us, length us, event | category | flops | bytes accessed | tf_op | source)
XLA Modules:
  0.0 87.1 jit_solution(2666184498356501583)
XLA Ops:
  0.6 85.8 %gated_moe_backward.1 = (bf16[512,256]{1,0:T(8,128)(2,1)S(1)}, bf16[64,256]{1,0:T(8,128)(2,1)S(1)}, f32[16,256]{1,0:T(8,128)S(1)}) custom-call(bf16[64,256]{1,0:T(8,128)(2,1)} %cot_hbm.1, bf16[64,256]{1,0:T(8,128)(2,1)} %act_hbm.1, f32[16,64]{1,0:T(8,128)} %bitcast.4, bf16[512,256]{1,0:T(8,128)(2,1)} %saved_hbm.1, bf16[256,4096]{1,0:T(8,128)(2,1)} %w_hbm.1, ...), custom_call_target="tpu_custom_call" | custom-call | flops 1073741824 | bytes 4194304 | tf_op jit(solution)/shard_map/gated_moe_backward/pallas_call | solution.py:548
  86.4 0.7 write_gradients.1
